TPU v7x, 32 devices: a whole 2x2x4 slice. The times are simulated.
32 devices in a mesh: dp: 4 (over z), space: 8 (over y, x, core).
Axes of the slice: x: 2, y: 2, z: 4, core: 2. Of those that a mesh axis runs over, the one named last changes fastest.
Arguments:
- features: bfloat16 [4, 32, 32, 32, 128], P('dp', None, 'space'), may hold values from -6 to 6
- cotangent: bfloat16 [4, 32, 32, 32, 128], P('dp', None, 'space'), may hold values from -6 to 6
- spectral: bfloat16 [256, 32, 2048], P('space', 'dp'), may hold values from -1.5 to 1.5
- pointwise: bfloat16 [32, 32], replicated, may hold values from -1 to 1
- biases: bfloat16 [32], replicated, may hold values from -3 to 3
Outputs:
- grad_input: bfloat16 [4, 32, 32, 32, 128], P('dp', None, 'space')
- grad_spectral: float32 [256, 32, 2048], P('space', 'dp')
All inputs are finite; a program needn't handle non-finite values.
Results may differ from a plain program's by a relative error of at most 0.025.
Values may be sent and summed in bfloat16 or wider, within the bound.
A program may use at most 128 MiB of HBM per device.

v0:
```python
import functools
import math

import jax
import jax.numpy as jnp
import ml_dtypes
import numpy as np
from jax import lax
from jax.experimental import pallas as pl
from jax.experimental.pallas import tpu as pltpu
from jax.sharding import PartitionSpec as P

KX = 32
KY = 32
KZ = 8


tanh_coef = 0.7978845608028654
cubic_coef = 0.044715


def frequencies(kept_count, length):
    indices = jnp.arange(kept_count, dtype=jnp.int32)
    return jnp.where(indices < kept_count // 2, indices, indices + (length - kept_count))


def plane_table(count_y, count_z, kept_y, kept_z):
    freq_y = frequencies(kept_y, count_y)
    freq_z = jnp.arange(kept_z, dtype=jnp.int32)
    turn_y = jnp.arange(count_y, dtype=jnp.int32)[:, None] * freq_y[None, :] % count_y
    turn_z = jnp.arange(count_z, dtype=jnp.int32)[:, None] * freq_z[None, :] % count_z
    angles = (
        2.0
        * math.pi
        * (
            turn_y[:, None, :, None].astype(jnp.float32) / count_y
            + turn_z[None, :, None, :].astype(jnp.float32) / count_z
        )
    )
    factor = 1.0 / math.sqrt(count_y * count_z)
    basis_table = jnp.stack([factor * jnp.cos(angles), -factor * jnp.sin(angles)], axis=-1)
    return basis_table.reshape(count_y * count_z, kept_y * kept_z, 2).astype(jnp.bfloat16)


def line_table(full_length, kept_count):
    freq_x = frequencies(kept_count, full_length)
    turns = jnp.arange(full_length, dtype=jnp.int32)[:, None] * freq_x[None, :] % full_length
    angles = 2.0 * math.pi * turns.astype(jnp.float32) / full_length
    factor = 1.0 / math.sqrt(full_length)
    cos_part = factor * jnp.cos(angles)
    sine_part = factor * jnp.sin(angles)
    first_row = jnp.stack([cos_part, -sine_part], axis=1)
    second = jnp.stack([sine_part, cos_part], axis=1)
    return jnp.stack([first_row, second], axis=0).astype(jnp.bfloat16)


def mode_doubling(kept_y, kept_z):
    mode_index = jnp.arange(kept_y * kept_z, dtype=jnp.int32) % kept_z
    return jnp.where(mode_index == 0, 1.0, 2.0).astype(jnp.float32)


def gelu_slope(values):
    inner_arg = tanh_coef * (values + cubic_coef * values * values * values)
    tanh_part = jnp.tanh(inner_arg)
    return 0.5 * (1.0 + tanh_part) + 0.5 * values * (1.0 - tanh_part * tanh_part) * tanh_coef * (
        1.0 + 3.0 * cubic_coef * values * values
    )


def product(equation, left_op, right_op):
    return jnp.einsum(equation, left_op, right_op, preferred_element_type=jnp.float32)


def forward_lines(coarse, line_basis):
    return product("xpscm,pxqk->kqscm", coarse, line_basis).astype(jnp.bfloat16)


def inverse_lines(spectrum, line_basis):
    return product("kqscm,pxqk->xpscm", spectrum, line_basis).astype(jnp.bfloat16)


def spectral_mix(spectrum, weights):
    real_part = spectrum[:, 0]
    imag_part = spectrum[:, 1]
    w_real = weights[:, :, 0]
    w_imag = weights[:, :, 1]
    out_real = product("ksim,mkio->ksom", real_part, w_real) - product(
        "ksim,mkio->ksom", imag_part, w_imag
    )
    out_imag = product("ksim,mkio->ksom", real_part, w_imag) + product(
        "ksim,mkio->ksom", imag_part, w_real
    )
    return jnp.stack([out_real, out_imag], axis=1).astype(jnp.bfloat16)


def spectral_pull(adjoint, weights):
    real_part = adjoint[:, 0]
    imag_part = adjoint[:, 1]
    w_real = weights[:, :, 0]
    w_imag = weights[:, :, 1]
    out_real = product("ksom,mkio->ksim", real_part, w_real) + product(
        "ksom,mkio->ksim", imag_part, w_imag
    )
    out_imag = product("ksom,mkio->ksim", imag_part, w_real) - product(
        "ksom,mkio->ksim", real_part, w_imag
    )
    return jnp.stack([out_real, out_imag], axis=1).astype(jnp.bfloat16)


def weight_grad(spectrum, adjoint):
    spec_real = spectrum[:, 0]
    spec_imag = spectrum[:, 1]
    adj_real = adjoint[:, 0]
    adj_imag = adjoint[:, 1]
    grad_real = product("ksim,ksom->mkio", spec_real, adj_real) + product(
        "ksim,ksom->mkio", spec_imag, adj_imag
    )
    grad_imag = product("ksim,ksom->mkio", spec_real, adj_imag) - product(
        "ksim,ksom->mkio", spec_imag, adj_real
    )
    return jnp.stack([grad_real, grad_imag], axis=2)


def to_modes(coarse):
    return lax.all_to_all(coarse, "space", split_axis=4, concat_axis=0, tiled=True)


def to_cells(returned):
    return lax.all_to_all(returned, "space", split_axis=0, concat_axis=4, tiled=True)


def plain_body(features, cotangent, spectral, pointwise, biases):
    samples, channels, slab_cells, span_y, span_z = features.shape
    full_length = slab_cells * lax.axis_size("space")
    plane_basis = plane_table(span_y, span_z, KY, KZ)
    line_basis = line_table(full_length, KX)
    doubling = mode_doubling(KY, KZ)
    doubling_cells = doubling.astype(jnp.bfloat16)[None, None, None, None, :]
    flat_cells = features.reshape(samples, channels, slab_cells, span_y * span_z)
    coarse = product("scxq,qmp->xpscm", flat_cells, plane_basis).astype(jnp.bfloat16)
    spectrum = forward_lines(to_modes(coarse), line_basis)
    local_modes = spectral.shape[0]
    blocks = lax.all_gather(spectral, "dp", axis=1, tiled=True)
    weights = blocks.reshape(local_modes, blocks.shape[1], 2, channels, channels)
    mixed_modes = spectral_mix(spectrum, weights)
    returned = to_cells(inverse_lines(mixed_modes, line_basis))
    spectral_part = product("xpscm,qmp->scxq", returned * doubling_cells, plane_basis)
    linear = product("sicq,io->socq", flat_cells, pointwise)
    pre_act = linear + biases.astype(jnp.float32)[None, :, None, None] + spectral_part
    upstream_grad = cotangent.reshape(flat_cells.shape).astype(jnp.float32)
    delta_cells = (upstream_grad * gelu_slope(pre_act)).astype(jnp.bfloat16)
    coarse_back = (
        product("scxq,qmp->xpscm", delta_cells, plane_basis) * doubling[None, None, None, None, :]
    ).astype(jnp.bfloat16)
    adjoint = forward_lines(to_modes(coarse_back), line_basis)
    pulled = spectral_pull(adjoint, weights)
    grad_terms = weight_grad(spectrum, adjoint)
    grad_spectral = lax.psum_scatter(
        grad_terms.reshape(local_modes, KX, 2 * channels * channels).astype(jnp.bfloat16),
        "dp",
        scatter_dimension=1,
        tiled=True,
    ).astype(jnp.float32)
    back_cells = to_cells(inverse_lines(pulled, line_basis))
    grad_cells = product("socq,io->sicq", delta_cells, pointwise) + product(
        "xpscm,qmp->scxq", back_cells, plane_basis
    )
    grad_input = grad_cells.astype(jnp.bfloat16).reshape(features.shape)
    return (grad_input, grad_spectral)


def np_frequencies(kept_count, length):
    indices = np.arange(kept_count)
    return np.where(indices < kept_count // 2, indices, indices + (length - kept_count))


def np_plane_rows(count_y, count_z, blocks, tiles, quads):
    turn_y = np.arange(count_y)[:, None] * np_frequencies(KY, count_y)[None, :] % count_y
    turn_z = np.arange(count_z)[:, None] * np.arange(KZ)[None, :] % count_z
    angles = 2.0 * np.pi * (
        turn_y[:, None, :, None] / count_y + turn_z[None, :, None, :] / count_z
    )
    factor = 1.0 / math.sqrt(count_y * count_z)
    table = np.stack([factor * np.cos(angles), -factor * np.sin(angles)], axis=0)
    table = table.reshape(2, count_y * count_z, blocks, tiles, quads)
    rows = table.transpose(4, 2, 0, 3, 1).reshape(-1, count_y * count_z)
    doubling = np.where(np.arange(KY * KZ) % KZ == 0, 1.0, 2.0).reshape(blocks, 1, tiles, quads)
    doubling = np.broadcast_to(doubling, (blocks, 2, tiles, quads)).transpose(3, 0, 1, 2)
    return rows.astype(ml_dtypes.bfloat16), doubling.reshape(-1, 1).astype(np.float32)


def np_line(full_length, blocks, owners):
    turns = np.arange(full_length)[:, None] * np_frequencies(KX, full_length)[None, :] % full_length
    angles = 2.0 * np.pi * turns / full_length
    factor = 1.0 / math.sqrt(full_length)
    cos_part, sine_part = factor * np.cos(angles), factor * np.sin(angles)
    table = np.stack(
        [np.stack([cos_part, -sine_part], 0), np.stack([sine_part, cos_part], 0)], 0
    )
    table = table.reshape(2, 2, blocks, full_length // blocks, owners, KX // owners)
    table = table.transpose(4, 1, 5, 2, 0, 3).reshape(2 * KX, 2 * full_length)
    return table.astype(ml_dtypes.bfloat16)


def np_selectors(channels, slab, quads):
    def one_hot(rows, columns, count_rows, count_columns):
        table = np.zeros((count_rows, count_columns), ml_dtypes.bfloat16)
        table[rows.reshape(-1), columns.reshape(-1)] = 1
        return table

    lanes = quads * channels
    j, c, x = np.meshgrid(np.arange(quads), np.arange(channels), np.arange(slab), indexing="ij")
    regroup = one_hot(
        (j * channels + c) * slab + x, (x * quads + j) * channels + c, lanes * slab, lanes * slab
    )
    j, i, o = np.meshgrid(
        np.arange(quads), np.arange(channels), np.arange(channels), indexing="ij"
    )
    spread = one_hot(
        j * channels + i,
        j * channels * channels + i * channels + o,
        lanes,
        quads * channels * channels,
    )
    spread = spread.reshape(lanes, quads, channels * channels).transpose(1, 0, 2)
    j, i, o = np.meshgrid(np.arange(quads), np.arange(quads), np.arange(channels), indexing="ij")
    tile = one_hot((j * quads + i) * channels + o, j * channels + o, quads * lanes, lanes)
    return regroup, np.ascontiguousarray(spread), tile


f32, bf16 = jnp.float32, jnp.bfloat16
NT = (((1,), (1,)), ((), ()))


def dot(left, right):
    return jnp.dot(left, right, preferred_element_type=f32)


def dot_nt(left, right):
    return lax.dot_general(left, right, NT, preferred_element_type=f32)


def start_exchange(axis, count, send, recv, send_sem, recv_sem):
    me = lax.axis_index(axis)
    copies = []
    for step in range(1, count):
        peer = lax.rem(me + step, count)
        copy = pltpu.make_async_remote_copy(
            src_ref=send.at[peer],
            dst_ref=recv.at[me],
            send_sem=send_sem.at[step],
            recv_sem=recv_sem.at[step],
            device_id={axis: peer},
            device_id_type=pl.DeviceIdType.MESH,
        )
        copy.start()
        copies.append(copy)
    recv[me] = send[me]
    return copies


def wait_all(copies):
    for copy in copies:
        copy.wait()


def layer_kernel(
    sizes,
    feats, cot, weights, mix_fwd, mix_back, bias, plane, doubling, line, regroup, spread, tile,
    out_input, out_spectral,
    coarse_acc, delta, spec_wide, adj_wide, cells, volume,
    space_send, space_recv, dp_send, dp_recv,
    space_ssem, space_rsem, dp_ssem, dp_rsem,
):
    blocks, owners, channels, slab, tiles, quads, kept = sizes
    lanes = quads * channels
    rows = 2 * kept * owners
    cells_count = feats.shape[1]
    chunk = 512
    chunks = cells_count // chunk
    group = blocks * 2 * 8
    mesh_id = pl.DeviceIdType.MESH

    barrier = pltpu.get_barrier_semaphore()
    for axis, count in (("space", blocks), ("dp", owners)):
        me = lax.axis_index(axis)
        for step in range(1, count):
            pl.semaphore_signal(
                barrier, inc=1, device_id={axis: lax.rem(me + step, count)}, device_id_type=mesh_id
            )
    pl.semaphore_wait(barrier, blocks + owners - 2)

    def send_cells(turn, coarse):
        wide = jnp.concatenate(
            [coarse[j * group : (j + 1) * group].astype(bf16) for j in range(quads)], axis=1
        )
        wide = dot(wide, regroup[...])
        for block in range(blocks):
            parts = [
                wide[(block * 2 + p) * 8 : (block * 2 + p + 1) * 8, x * lanes : (x + 1) * lanes]
                for p in range(2)
                for x in range(slab)
            ]
            space_send[turn, block] = jnp.concatenate(parts, axis=0).astype(bf16)
        return start_exchange(
            "space", blocks, space_send.at[turn], space_recv.at[turn],
            space_ssem.at[turn], space_rsem.at[turn],
        )

    def cells_to_modes(turn, dp_turn):
        cells[...] = space_recv[turn].astype(f32).reshape(cells.shape)
        count = blocks * 2 * slab
        for t in range(tiles):
            column = cells[pl.ds(t, count, stride=8), :].astype(bf16)
            spectrum = dot(line[...], column).astype(bf16)
            dp_send[dp_turn, :, :, t * lanes : (t + 1) * lanes] = spectrum.reshape(
                owners, 2 * kept, lanes
            )
        return start_dp(dp_turn)

    def start_dp(turn):
        return start_exchange(
            "dp", owners, dp_send.at[turn], dp_recv.at[turn], dp_ssem.at[turn], dp_rsem.at[turn]
        )

    def modes_to_cells(dp_turn, turn):
        count = blocks * 2 * slab
        for t in range(tiles):
            column = dp_recv[dp_turn, :, :, t * lanes : (t + 1) * lanes].reshape(rows, lanes)
            back = lax.dot_general(
                line[...], column, (((0,), (0,)), ((), ())), preferred_element_type=f32
            )
            cells[pl.ds(t, count, stride=8), :] = back
        space_send[turn] = cells[...].astype(bf16).reshape(space_send.shape[1:])
        return start_exchange(
            "space", blocks, space_send.at[turn], space_recv.at[turn],
            space_ssem.at[turn], space_rsem.at[turn],
        )

    def receive_volume(turn, scaled):
        parts = []
        for block in range(blocks):
            held = space_recv[turn, block].astype(f32)
            for p in range(2):
                parts.append(
                    jnp.concatenate(
                        [held[(p * slab + x) * 8 : (p * slab + x + 1) * 8] for x in range(slab)],
                        axis=1,
                    )
                )
        wide = jnp.concatenate(parts, axis=0).astype(bf16)
        wide = dot_nt(wide, regroup[...])
        for j in range(quads):
            part = wide[:, j * lanes : (j + 1) * lanes]
            if scaled:
                part = part * doubling[j * group : (j + 1) * group]
            volume[:, j * group : (j + 1) * group] = part.T.astype(bf16)

    coarse_acc[...] = jnp.zeros_like(coarse_acc)

    def analyse(step, _):
        at = pl.ds(pl.multiple_of(step * chunk, chunk), chunk)
        coarse_acc[...] += dot_nt(plane[:, at], feats[:, at])
        return 0

    lax.fori_loop(0, chunks, analyse, 0)
    wait_all(send_cells(0, coarse_acc[...]))
    wait_all(cells_to_modes(0, 0))

    def mix(t, _):
        at = pl.ds(pl.multiple_of(t * lanes, lanes), lanes)
        column = dp_recv[0, :, :, at].reshape(rows, lanes)
        parts = []
        for j in range(quads):
            m = t * quads + j
            spec_wide[m] = dot(column, spread[j])
            total = [None] * (2 * owners)
            for s in range(channels * channels // 128):
                lo = s * 128
                w_re = weights[m, :, lo : lo + 128].astype(f32)
                lo2 = channels * channels + lo
                w_im = weights[m, :, lo2 : lo2 + 128].astype(f32)
                for n in range(owners):
                    re = spec_wide[m, 2 * n * kept : (2 * n + 1) * kept, lo : lo + 128]
                    im = spec_wide[m, (2 * n + 1) * kept : (2 * n + 2) * kept, lo : lo + 128]
                    out_re = re * w_re - im * w_im
                    out_im = re * w_im + im * w_re
                    total[2 * n] = out_re if s == 0 else total[2 * n] + out_re
                    total[2 * n + 1] = out_im if s == 0 else total[2 * n + 1] + out_im
            parts.append(jnp.concatenate(total, axis=0).astype(bf16))
        mixed = dot(jnp.concatenate(parts, axis=1), tile[...])
        dp_send[1, :, :, at] = mixed.astype(bf16).reshape(owners, 2 * kept, lanes)
        return 0

    lax.fori_loop(0, tiles, mix, 0)
    wait_all(start_dp(1))
    wait_all(modes_to_cells(1, 1))
    receive_volume(1, True)

    coarse_acc[...] = jnp.zeros_like(coarse_acc)

    def activate(step, _):
        at = pl.ds(pl.multiple_of(step * chunk, chunk), chunk)
        pre_act = dot(volume[...], plane[:, at]) + dot(mix_fwd[...], feats[:, at]) + bias[...]
        part = (cot[:, at].astype(f32) * gelu_slope(pre_act)).astype(bf16)
        delta[:, at] = part
        coarse_acc[...] += dot_nt(plane[:, at], part)
        return 0

    lax.fori_loop(0, chunks, activate, 0)
    wait_all(send_cells(2, coarse_acc[...] * doubling[...]))
    wait_all(cells_to_modes(2, 2))

    def pull(t, _):
        at = pl.ds(pl.multiple_of(t * lanes, lanes), lanes)
        column = dp_recv[2, :, :, at].reshape(rows, lanes)
        pulled = jnp.zeros((rows, lanes), f32)
        for j in range(quads):
            m = t * quads + j
            wide = dot_nt(column, tile[j * lanes : (j + 1) * lanes])
            adj_wide[m] = wide
            adjs = [wide[r * kept : (r + 1) * kept] for r in range(2 * owners)]
            products = []
            for s in range(channels * channels // 128):
                lo = s * 128
                w_re = weights[m, :, lo : lo + 128].astype(f32)
                lo2 = channels * channels + lo
                w_im = weights[m, :, lo2 : lo2 + 128].astype(f32)
                terms = []
                for n in range(owners):
                    re, im = adjs[2 * n], adjs[2 * n + 1]
                    terms += [re * w_re + im * w_im, im * w_re - re * w_im]
                products.append(jnp.concatenate(terms, axis=0).astype(bf16))
            pulled += dot_nt(jnp.concatenate(products, axis=1), spread[j])
        dp_send[3, :, :, at] = pulled.astype(bf16).reshape(owners, 2 * kept, lanes)
        return 0

    lax.fori_loop(0, tiles, pull, 0)
    copies = start_dp(3)

    def weight_terms(m, _):
        adjs = [adj_wide[m, r * kept : (r + 1) * kept] for r in range(2 * owners)]
        for s in range(channels * channels // 128):
            lo = s * 128
            grad_re, grad_im = None, None
            for n in range(owners):
                re = spec_wide[m, 2 * n * kept : (2 * n + 1) * kept, lo : lo + 128]
                im = spec_wide[m, (2 * n + 1) * kept : (2 * n + 2) * kept, lo : lo + 128]
                a_re, a_im = adjs[2 * n], adjs[2 * n + 1]
                term_re = re * a_re + im * a_im
                term_im = re * a_im - im * a_re
                grad_re = term_re if n == 0 else grad_re + term_re
                grad_im = term_im if n == 0 else grad_im + term_im
            out_spectral[m, :, lo : lo + 128] = grad_re
            lo2 = channels * channels + lo
            out_spectral[m, :, lo2 : lo2 + 128] = grad_im
        return 0

    lax.fori_loop(0, tiles * quads, weight_terms, 0)
    wait_all(copies)
    wait_all(modes_to_cells(3, 3))
    receive_volume(3, False)

    def finish(step, _):
        at = pl.ds(pl.multiple_of(step * chunk, chunk), chunk)
        grad = dot(volume[...], plane[:, at]) + dot(mix_back[...], delta[:, at])
        out_input[:, at] = grad.astype(bf16)
        return 0

    lax.fori_loop(0, chunks, finish, 0)


def fits(features, spectral, owners):
    samples, channels, slab = features.shape[:3]
    modes, kept = spectral.shape[:2]
    return (
        samples == 1 and kept == 8 and channels == 32 and slab == 4
        and modes == 32 and (2 * kept * owners) % 16 == 0
    )


def body(features, cotangent, spectral, pointwise, biases):
    blocks, owners = lax.axis_size("space"), lax.axis_size("dp")
    if not fits(features, spectral, owners):
        return plain_body(features, cotangent, spectral, pointwise, biases)
    _, channels, slab, span_y, span_z = features.shape
    modes, kept = spectral.shape[:2]
    tiles = 8
    quads = modes // tiles
    lanes = quads * channels
    cell_rows, cells_count = channels * slab, span_y * span_z
    plane, doubling = np_plane_rows(span_y, span_z, blocks, tiles, quads)
    line = np_line(slab * blocks, blocks, owners)
    regroup, spread, tile = np_selectors(channels, slab, quads)
    eye = jnp.eye(slab, dtype=bf16)
    mix_back = jnp.einsum("io,xy->ixoy", pointwise, eye).reshape(cell_rows, cell_rows)
    mix_fwd = jnp.einsum("io,xy->oxiy", pointwise, eye).reshape(cell_rows, cell_rows)
    bias = jnp.repeat(biases.astype(f32), slab)[:, None]
    plane_rows = plane.shape[0]
    sizes = (blocks, owners, channels, slab, tiles, quads, kept)
    vmem = pl.BlockSpec(memory_space=pltpu.VMEM)
    grad_input, grad_spectral = pl.pallas_call(
        functools.partial(layer_kernel, sizes),
        out_shape=(
            jax.ShapeDtypeStruct((cell_rows, cells_count), bf16),
            jax.ShapeDtypeStruct(spectral.shape, f32),
        ),
        in_specs=[vmem] * 12,
        out_specs=(vmem, vmem),
        scratch_shapes=[
            pltpu.VMEM((plane_rows, cell_rows), f32),
            pltpu.VMEM((cell_rows, cells_count), bf16),
            pltpu.VMEM((modes, 2 * kept * owners, channels * channels), f32),
            pltpu.VMEM((modes, 2 * kept * owners, 128), f32),
            pltpu.VMEM((blocks * 2 * slab * 8, lanes), f32),
            pltpu.VMEM((cell_rows, plane_rows), bf16),
            pltpu.VMEM((4, blocks, 2 * slab * 8, lanes), bf16),
            pltpu.VMEM((4, blocks, 2 * slab * 8, lanes), bf16),
            pltpu.VMEM((4, owners, 2 * kept, modes * channels), bf16),
            pltpu.VMEM((4, owners, 2 * kept, modes * channels), bf16),
            pltpu.SemaphoreType.DMA((4, blocks)),
            pltpu.SemaphoreType.DMA((4, blocks)),
            pltpu.SemaphoreType.DMA((4, owners)),
            pltpu.SemaphoreType.DMA((4, owners)),
        ],
        compiler_params=pltpu.CompilerParams(
            collective_id=0, has_side_effects=True, vmem_limit_bytes=56 * 1024 * 1024
        ),
    )(
        features.reshape(cell_rows, cells_count),
        cotangent.reshape(cell_rows, cells_count),
        spectral, mix_fwd, mix_back, bias,
        plane, doubling, line, regroup, spread, tile,
    )
    return grad_input.reshape(features.shape), grad_spectral


def solution(mesh):
    placed = (
        P("dp", None, "space", None, None),
        P("dp", None, "space", None, None),
        P("space", "dp", None),
        P(),
        P(),
    )
    return jax.shard_map(
        body,
        mesh=mesh,
        in_specs=placed,
        out_specs=(P("dp", None, "space", None, None), P("space", "dp", None)),
        check_vma=False,
    )
```

profile of v0, /device:TPU:0, one launch (start us, length us, event | category | flops | bytes accessed | tf_op | source)
XLA Modules:
  0.0 82.1 jit_solution(13154656584108168912)
XLA Ops:
  0.6 0.7 broadcast_in_dim.3
  1.4 0.7 broadcast_in_dim_reshape.4.bias
  2.1 0.9 %multiply_bitcast_fusion = (bf16[32,4,32,4]{3,2,1,0:T(8,128)(2,1)S(1)}, bf16[32,4,32,4]{3,0,1,2:T(8,128)(2,1)S(1)}) fusion(bf16[32,32]{1,0:T(8,128)(2,1)} %param.14, bf16[4,4]{1,0:T(4,128)(2,1)S(1)} %fusion), kind=kLoop, calls=%fused_computation | loop fusion | flops 16384 | bytes 67616 | tf_op jit(solution)/shard_map/io,xy->ixoy/transpose | solution.py:496
  3.0 0.0 copy-start.1
  3.0 2.6 %reshape.22.mix_back = bf16[128,128]{1,0:T(8,128)(2,1)} reshape(bf16[32,4,32,4]{3,2,1,0:T(8,128)(2,1)S(1)} %get-tuple-element.6) | data formatting | bytes 65536 | tf_op jit(solution)/shard_map/reshape | solution.py:496
  5.6 0.7 copy.15
  6.2 2.5 %reshape.21.mix_fwd = bf16[128,128]{1,0:T(8,128)(2,1)} reshape(bf16[32,4,32,4]{3,2,1,0:T(8,128)(2,1)S(1)} %copy.15) | data formatting | bytes 65536 | tf_op jit(solution)/shard_map/reshape | solution.py:497
  8.8 0.0 copy-done.1
  8.8 3.5 %copy_bitcast_fusion = (bf16[128,4096]{1,0:T(8,128)(2,1)}, bf16[128,4096]{1,0:T(8,128)(2,1)}) fusion(bf16[16,8,32,128]{3,2,1,0:T(8,128)(2,1)S(1)} %bitcast.21, bf16[16,8,32,128]{3,2,1,0:T(8,128)(2,1)} %bitcast.22), kind=kLoop, calls=%fused_computation.2 | loop fusion | bytes 4194304 | tf_op jit(solution)/shard_map/reshape | solution.py:531
  12.3 65.9 %shard_map.122 = (bf16[128,4096]{1,0:T(8,128)(2,1)}, f32[32,8,2048]{2,1,0:T(8,128)}) custom-call(bf16[128,4096]{1,0:T(8,128)(2,1)} %get-tuple-element.9.feats, bf16[128,4096]{1,0:T(8,128)(2,1)} %get-tuple-element.8.cot, bf16[32,8,2048]{2,1,0:T(8,128)(2,1)} %weights.1, bf16[128,128]{1,0:T(8,128)(2,1)} %reshape.21.mix_fwd, bf16[128,128]{1,0:T(8,128)(2,1)} %reshape.22.mix_back, ...), custom_call_target="tpu_custom_call" | custom-call | tf_op jit(solution)/shard_map/pallas_call | solution.py:502
  78.2 0.0 copy-start
  78.2 2.6 %copy.19 = bf16[16,8,32,128]{3,2,1,0:T(8,128)(2,1)} copy(bf16[16,8,32,128]{3,1,2,0:T(8,128)(2,1)} %bitcast.19) | data formatting | bytes 2097152
  80.8 0.0 copy-done
  80.8 1.3 %copy.23 = f32[32,8,2048]{2,1,0:T(8,128)} copy(f32[32,8,2048]{2,1,0:T(8,128)S(1)} %copy-done) | data formatting | bytes 4194304
  (1 shorter events, 0.0 us)
Async XLA Ops:
  3.0 5.8 %copy-start.1 = (bf16[1,32,4,32,128]{4,3,2,1,0:T(8,128)(2,1)S(1)}, bf16[1,32,4,32,128]{4,3,2,1,0:T(8,128)(2,1)}, u32[]{:S(2)}) copy-start(bf16[1,32,4,32,128]{4,3,2,1,0:T(8,128)(2,1)} %param.12) | copy-start | bytes 3145732
  78.2 2.6 %copy-start = (f32[32,8,2048]{2,1,0:T(8,128)S(1)}, f32[32,8,2048]{2,1,0:T(8,128)}, u32[]{:S(2)}) copy-start(f32[32,8,2048]{2,1,0:T(8,128)} %get-tuple-element.13) | copy-start | bytes 6291460
where the time goes:
time: 82.3 us; the launch traced here: 82.1 us
  Pallas kernels  65.9 us (80%)
  local copies, waits for them, and re-layouts  14.6 us (18%)
  other arithmetic  0.91 us (1%)
    pallas_call x1, Pallas kernels, body(): pl.pallas_call(functools.partial(layer_kernel, sizes), out_shape=(jax.Sha...  65.9 us
    unnamed x6, local copies, waits for them, and re-layouts  3.9 us
    reshape x1, local copies, waits for them, and re-layouts, body(): cotangent.reshape(cell_rows, cells_count)  3.47 us
    reshape x1, local copies, waits for them, and re-layouts, body(): jnp.einsum('io,xy->ixoy', pointwise, eye).reshape(cell_rows, cell_rows)  2.56 us
    reshape x1, local copies, waits for them, and re-layouts, body(): jnp.einsum('io,xy->oxiy', pointwise, eye).reshape(cell_rows, cell_rows)  2.55 us

commit v1 on v0

--- a/solution.py
+++ b/solution.py
@@ -225,11 +225,16 @@
     spread = spread.reshape(lanes, quads, channels * channels).transpose(1, 0, 2)
     j, i, o = np.meshgrid(np.arange(quads), np.arange(quads), np.arange(channels), indexing="ij")
     tile = one_hot((j * quads + i) * channels + o, j * channels + o, quads * lanes, lanes)
-    return regroup, np.ascontiguousarray(spread), tile
+    cells = np.arange(channels * slab)
+    repeat = one_hot(cells, cells // slab, channels * slab, channels)
+    flat = np.ascontiguousarray
+    return regroup, flat(spread), flat(spread.transpose(0, 2, 1)), tile, flat(tile.T), repeat
 
 
 f32, bf16 = jnp.float32, jnp.bfloat16
 NT = (((1,), (1,)), ((), ()))
+TN = (((0,), (0,)), ((), ()))
+HALVES = 2
 
 
 def dot(left, right):
@@ -266,20 +271,45 @@
 
 def layer_kernel(
     sizes,
-    feats, cot, weights, mix_fwd, mix_back, bias, plane, doubling, line, regroup, spread, tile,
+    feats, cot_hbm, weights_hbm, pointwise, biases, analysis_hbm, synthesis_hbm,
+    doubling, line, regroup, spread, gather, tile, untile, repeat,
     out_input, out_spectral,
-    coarse_acc, delta, spec_wide, adj_wide, cells, volume,
+    cot, weights, analysis, synthesis, grads,
+    natural, rows_in, delta, coarse_acc, volume, mix_fwd, mix_back, bias,
+    stack, parts, spec_wide, adj_wide, products, pulled, cells,
     space_send, space_recv, dp_send, dp_recv,
-    space_ssem, space_rsem, dp_ssem, dp_rsem,
+    load_sem, analysis_sem, space_ssem, space_rsem, dp_ssem, dp_rsem,
 ):
-    blocks, owners, channels, slab, tiles, quads, kept = sizes
+    blocks, owners, channels, slab, span_y, tiles, quads, kept = sizes
     lanes = quads * channels
     rows = 2 * kept * owners
-    cells_count = feats.shape[1]
-    chunk = 512
+    cell_rows = channels * slab
+    width = feats.shape[1]
+    cells_count = span_y * width
+    chunk = analysis_hbm.shape[0] // analysis_sem.shape[0]
     chunks = cells_count // chunk
-    group = blocks * 2 * 8
+    lines = chunk // width
+    group = blocks * 2 * tiles
+    near = tiles // HALVES
+    square = channels * channels
     mesh_id = pl.DeviceIdType.MESH
+
+    analysis_loads = [
+        pltpu.make_async_copy(
+            analysis_hbm.at[pl.ds(step * chunk, chunk)],
+            analysis.at[pl.ds(step * chunk, chunk)],
+            analysis_sem.at[step],
+        )
+        for step in range(chunks)
+    ]
+    for copy in analysis_loads:
+        copy.start()
+    load_cot = pltpu.make_async_copy(cot_hbm, cot, load_sem.at[0])
+    load_weights = pltpu.make_async_copy(weights_hbm, weights, load_sem.at[1])
+    load_synthesis = pltpu.make_async_copy(synthesis_hbm, synthesis, load_sem.at[2])
+    load_cot.start()
+    load_weights.start()
+    load_synthesis.start()
 
     barrier = pltpu.get_barrier_semaphore()
     for axis, count in (("space", blocks), ("dp", owners)):
@@ -288,194 +318,284 @@
             pl.semaphore_signal(
                 barrier, inc=1, device_id={axis: lax.rem(me + step, count)}, device_id_type=mesh_id
             )
-    pl.semaphore_wait(barrier, blocks + owners - 2)
+
+    def widen(source):
+        def some(step, _):
+            at = pl.ds(pl.multiple_of(step * 512, 512), 512)
+            natural[at, :] = source[at, :].astype(f32)
+            return 0
+
+        lax.fori_loop(0, natural.shape[0] // 512, some, 0)
+
+    def plane_lines(step):
+        return jnp.concatenate(
+            [natural[pl.ds(step * lines + u, cell_rows, stride=span_y), :] for u in range(lines)],
+            axis=1,
+        )
+
+    def columns(step):
+        return pl.ds(pl.multiple_of(step * chunk, chunk), chunk)
+
+    def send_space(turn):
+        return start_exchange(
+            "space", blocks, space_send.at[turn], space_recv.at[turn],
+            space_ssem.at[turn], space_rsem.at[turn],
+        )
+
+    def send_dp(turn, half):
+        at = turn * HALVES + half
+        return start_exchange(
+            "dp", owners, dp_send.at[at], dp_recv.at[at], dp_ssem.at[at], dp_rsem.at[at]
+        )
 
     def send_cells(turn, coarse):
         wide = jnp.concatenate(
-            [coarse[j * group : (j + 1) * group].astype(bf16) for j in range(quads)], axis=1
+            [coarse[:, j * group : (j + 1) * group].T.astype(bf16) for j in range(quads)], axis=1
         )
         wide = dot(wide, regroup[...])
         for block in range(blocks):
-            parts = [
-                wide[(block * 2 + p) * 8 : (block * 2 + p + 1) * 8, x * lanes : (x + 1) * lanes]
+            pieces = [
+                wide[
+                    (block * 2 + p) * tiles : (block * 2 + p + 1) * tiles,
+                    x * lanes : (x + 1) * lanes,
+                ]
                 for p in range(2)
                 for x in range(slab)
             ]
-            space_send[turn, block] = jnp.concatenate(parts, axis=0).astype(bf16)
-        return start_exchange(
-            "space", blocks, space_send.at[turn], space_recv.at[turn],
-            space_ssem.at[turn], space_rsem.at[turn],
-        )
+            space_send[turn, block] = jnp.concatenate(pieces, axis=0).astype(bf16)
+        return send_space(turn)
 
     def cells_to_modes(turn, dp_turn):
         cells[...] = space_recv[turn].astype(f32).reshape(cells.shape)
-        count = blocks * 2 * slab
-        for t in range(tiles):
-            column = cells[pl.ds(t, count, stride=8), :].astype(bf16)
-            spectrum = dot(line[...], column).astype(bf16)
-            dp_send[dp_turn, :, :, t * lanes : (t + 1) * lanes] = spectrum.reshape(
-                owners, 2 * kept, lanes
-            )
-        return start_dp(dp_turn)
-
-    def start_dp(turn):
-        return start_exchange(
-            "dp", owners, dp_send.at[turn], dp_recv.at[turn], dp_ssem.at[turn], dp_rsem.at[turn]
-        )
-
-    def modes_to_cells(dp_turn, turn):
-        count = blocks * 2 * slab
-        for t in range(tiles):
-            column = dp_recv[dp_turn, :, :, t * lanes : (t + 1) * lanes].reshape(rows, lanes)
-            back = lax.dot_general(
-                line[...], column, (((0,), (0,)), ((), ())), preferred_element_type=f32
-            )
-            cells[pl.ds(t, count, stride=8), :] = back
+        copies = []
+        for half in range(HALVES):
+            wide = jnp.concatenate(
+                [
+                    cells[pl.ds(half * near + t, blocks * 2 * slab, stride=tiles), :]
+                    for t in range(near)
+                ],
+                axis=1,
+            ).astype(bf16)
+            spectrum = dot(line[...], wide).astype(bf16)
+            dp_send[dp_turn * HALVES + half] = spectrum.reshape(owners, 2 * kept, near * lanes)
+            copies.append(send_dp(dp_turn, half))
+        return copies
+
+    def modes_to_cells(dp_turn, turn, copies):
+        for half in range(HALVES):
+            wait_all(copies[half])
+            wide = dp_recv[dp_turn * HALVES + half].reshape(rows, near * lanes)
+            back = lax.dot_general(line[...], wide, TN, preferred_element_type=f32)
+            for t in range(near):
+                cells[pl.ds(half * near + t, blocks * 2 * slab, stride=tiles), :] = back[
+                    :, t * lanes : (t + 1) * lanes
+                ]
         space_send[turn] = cells[...].astype(bf16).reshape(space_send.shape[1:])
-        return start_exchange(
-            "space", blocks, space_send.at[turn], space_recv.at[turn],
-            space_ssem.at[turn], space_rsem.at[turn],
-        )
+        return send_space(turn)
 
     def receive_volume(turn, scaled):
-        parts = []
+        pieces = []
         for block in range(blocks):
             held = space_recv[turn, block].astype(f32)
             for p in range(2):
-                parts.append(
+                pieces.append(
                     jnp.concatenate(
-                        [held[(p * slab + x) * 8 : (p * slab + x + 1) * 8] for x in range(slab)],
+                        [
+                            held[(p * slab + x) * tiles : (p * slab + x + 1) * tiles]
+                            for x in range(slab)
+                        ],
                         axis=1,
                     )
                 )
-        wide = jnp.concatenate(parts, axis=0).astype(bf16)
-        wide = dot_nt(wide, regroup[...])
+        wide = dot_nt(jnp.concatenate(pieces, axis=0).astype(bf16), regroup[...])
         for j in range(quads):
-            part = wide[:, j * lanes : (j + 1) * lanes]
+            part = wide[:, j * lanes : (j + 1) * lanes].T
             if scaled:
-                part = part * doubling[j * group : (j + 1) * group]
-            volume[:, j * group : (j + 1) * group] = part.T.astype(bf16)
-
+                part = part * doubling[:, j * group : (j + 1) * group]
+            volume[:, j * group : (j + 1) * group] = part.astype(bf16)
+
+    def stack_half(dp_turn, half):
+        for t in range(near):
+            stack[t * rows : (t + 1) * rows] = dp_recv[
+                dp_turn * HALVES + half, :, :, t * lanes : (t + 1) * lanes
+            ].reshape(rows, lanes)
+
+    def unstack_half(dp_turn, half, values):
+        for t in range(near):
+            dp_send[dp_turn * HALVES + half, :, :, t * lanes : (t + 1) * lanes] = (
+                values[t * rows : (t + 1) * rows].astype(bf16).reshape(owners, 2 * kept, lanes)
+            )
+        return send_dp(dp_turn, half)
+
+    def weight_tiles(m, s):
+        lo = s * 128
+        return (
+            weights[m, :, lo : lo + 128].astype(f32),
+            weights[m, :, square + lo : square + lo + 128].astype(f32),
+        )
+
+    widen(feats)
     coarse_acc[...] = jnp.zeros_like(coarse_acc)
-
-    def analyse(step, _):
-        at = pl.ds(pl.multiple_of(step * chunk, chunk), chunk)
-        coarse_acc[...] += dot_nt(plane[:, at], feats[:, at])
-        return 0
-
-    lax.fori_loop(0, chunks, analyse, 0)
-    wait_all(send_cells(0, coarse_acc[...]))
-    wait_all(cells_to_modes(0, 0))
-
-    def mix(t, _):
-        at = pl.ds(pl.multiple_of(t * lanes, lanes), lanes)
-        column = dp_recv[0, :, :, at].reshape(rows, lanes)
-        parts = []
-        for j in range(quads):
-            m = t * quads + j
-            spec_wide[m] = dot(column, spread[j])
-            total = [None] * (2 * owners)
-            for s in range(channels * channels // 128):
-                lo = s * 128
-                w_re = weights[m, :, lo : lo + 128].astype(f32)
-                lo2 = channels * channels + lo
-                w_im = weights[m, :, lo2 : lo2 + 128].astype(f32)
-                for n in range(owners):
-                    re = spec_wide[m, 2 * n * kept : (2 * n + 1) * kept, lo : lo + 128]
-                    im = spec_wide[m, (2 * n + 1) * kept : (2 * n + 2) * kept, lo : lo + 128]
-                    out_re = re * w_re - im * w_im
-                    out_im = re * w_im + im * w_re
-                    total[2 * n] = out_re if s == 0 else total[2 * n] + out_re
-                    total[2 * n + 1] = out_im if s == 0 else total[2 * n + 1] + out_im
-            parts.append(jnp.concatenate(total, axis=0).astype(bf16))
-        mixed = dot(jnp.concatenate(parts, axis=1), tile[...])
-        dp_send[1, :, :, at] = mixed.astype(bf16).reshape(owners, 2 * kept, lanes)
-        return 0
-
-    lax.fori_loop(0, tiles, mix, 0)
-    wait_all(start_dp(1))
-    wait_all(modes_to_cells(1, 1))
+    for step in range(chunks):
+        analysis_loads[step].wait()
+        part = plane_lines(step).astype(bf16)
+        rows_in[:, step * chunk : (step + 1) * chunk] = part
+        coarse_acc[...] += dot(part, analysis[step * chunk : (step + 1) * chunk, :])
+    pl.semaphore_wait(barrier, blocks + owners - 2)
+    copies = send_cells(0, coarse_acc[...])
+
+    same_cell = lax.rem(lax.broadcasted_iota(jnp.int32, mix_fwd.shape, 0), slab) == lax.rem(
+        lax.broadcasted_iota(jnp.int32, mix_fwd.shape, 1), slab
+    )
+    spread_out = dot_nt(dot_nt(repeat[...], pointwise[...]).astype(bf16), repeat[...])
+    mix_fwd[...] = jnp.where(same_cell, spread_out, 0.0).astype(bf16)
+    spread_out = dot_nt(dot(repeat[...], pointwise[...]).astype(bf16), repeat[...])
+    mix_back[...] = jnp.where(same_cell, spread_out, 0.0).astype(bf16)
+    bias[...] = jnp.sum(
+        repeat[...].astype(f32) * biases[...].astype(f32), axis=1, keepdims=True
+    )
+    load_cot.wait()
+    widen(cot)
+    wait_all(copies)
+    copies = cells_to_modes(0, 0)
+    load_weights.wait()
+
+    back_copies = []
+    for half in range(HALVES):
+        wait_all(copies[half])
+        stack_half(0, half)
+
+        def mix(j, _, half=half):
+            spec_wide[half, j] = dot(stack[...], spread[j])
+            for t in range(near):
+                m = (half * near + t) * quads + j
+                base = t * rows
+                total = [None] * (2 * owners)
+                for s in range(square // 128):
+                    lo = s * 128
+                    w_re, w_im = weight_tiles(m, s)
+                    for n in range(owners):
+                        at = base + 2 * n * kept
+                        re = spec_wide[half, j, at : at + kept, lo : lo + 128]
+                        im = spec_wide[half, j, at + kept : at + 2 * kept, lo : lo + 128]
+                        out_re = re * w_re - im * w_im
+                        out_im = re * w_im + im * w_re
+                        total[2 * n] = out_re if s == 0 else total[2 * n] + out_re
+                        total[2 * n + 1] = out_im if s == 0 else total[2 * n + 1] + out_im
+                parts[j, base : base + rows, :] = jnp.concatenate(total, axis=0).astype(bf16)
+            return 0
+
+        lax.fori_loop(0, quads, mix, 0)
+        mixed = dot(jnp.concatenate([parts[j] for j in range(quads)], axis=1), tile[...])
+        back_copies.append(unstack_half(1, half, mixed))
+    wait_all(modes_to_cells(1, 1, back_copies))
+    load_synthesis.wait()
     receive_volume(1, True)
 
     coarse_acc[...] = jnp.zeros_like(coarse_acc)
 
     def activate(step, _):
-        at = pl.ds(pl.multiple_of(step * chunk, chunk), chunk)
-        pre_act = dot(volume[...], plane[:, at]) + dot(mix_fwd[...], feats[:, at]) + bias[...]
-        part = (cot[:, at].astype(f32) * gelu_slope(pre_act)).astype(bf16)
+        at = columns(step)
+        pre_act = dot(volume[...], synthesis[:, at]) + dot(mix_fwd[...], rows_in[:, at]) + bias[...]
+        part = (plane_lines(step) * gelu_slope(pre_act)).astype(bf16)
         delta[:, at] = part
-        coarse_acc[...] += dot_nt(plane[:, at], part)
+        coarse_acc[...] += dot(part, analysis[at, :])
         return 0
 
     lax.fori_loop(0, chunks, activate, 0)
     wait_all(send_cells(2, coarse_acc[...] * doubling[...]))
-    wait_all(cells_to_modes(2, 2))
-
-    def pull(t, _):
-        at = pl.ds(pl.multiple_of(t * lanes, lanes), lanes)
-        column = dp_recv[2, :, :, at].reshape(rows, lanes)
-        pulled = jnp.zeros((rows, lanes), f32)
+    copies = cells_to_modes(2, 2)
+
+    back_copies = []
+    for half in range(HALVES):
+        wait_all(copies[half])
+        stack_half(2, half)
+        wide = dot(stack[...], untile[...])
         for j in range(quads):
-            m = t * quads + j
-            wide = dot_nt(column, tile[j * lanes : (j + 1) * lanes])
-            adj_wide[m] = wide
-            adjs = [wide[r * kept : (r + 1) * kept] for r in range(2 * owners)]
-            products = []
-            for s in range(channels * channels // 128):
-                lo = s * 128
-                w_re = weights[m, :, lo : lo + 128].astype(f32)
-                lo2 = channels * channels + lo
-                w_im = weights[m, :, lo2 : lo2 + 128].astype(f32)
-                terms = []
-                for n in range(owners):
-                    re, im = adjs[2 * n], adjs[2 * n + 1]
-                    terms += [re * w_re + im * w_im, im * w_re - re * w_im]
-                products.append(jnp.concatenate(terms, axis=0).astype(bf16))
-            pulled += dot_nt(jnp.concatenate(products, axis=1), spread[j])
-        dp_send[3, :, :, at] = pulled.astype(bf16).reshape(owners, 2 * kept, lanes)
+            adj_wide[half, j] = wide[:, j * lanes : (j + 1) * lanes]
+        pulled[...] = jnp.zeros_like(pulled)
+
+        def pull(j, _, half=half):
+            for t in range(near):
+                m = (half * near + t) * quads + j
+                base = t * rows
+                adjs = [
+                    adj_wide[half, j, base + r * kept : base + (r + 1) * kept]
+                    for r in range(2 * owners)
+                ]
+                for s in range(square // 128):
+                    w_re, w_im = weight_tiles(m, s)
+                    terms = []
+                    for n in range(owners):
+                        re, im = adjs[2 * n], adjs[2 * n + 1]
+                        terms += [re * w_re + im * w_im, im * w_re - re * w_im]
+                    products[base : base + rows, s * 128 : (s + 1) * 128] = jnp.concatenate(
+                        terms, axis=0
+                    ).astype(bf16)
+            pulled[...] += dot(products[...], gather[j])
+            return 0
+
+        lax.fori_loop(0, quads, pull, 0)
+        back_copies.append(unstack_half(3, half, pulled[...]))
+
+    for half in range(HALVES):
+
+        def weight_terms(j, _, half=half):
+            for t in range(near):
+                m = (half * near + t) * quads + j
+                base = t * rows
+                adjs = [
+                    adj_wide[half, j, base + r * kept : base + (r + 1) * kept]
+                    for r in range(2 * owners)
+                ]
+                for s in range(square // 128):
+                    lo = s * 128
+                    grad_re, grad_im = None, None
+                    for n in range(owners):
+                        at = base + 2 * n * kept
+                        re = spec_wide[half, j, at : at + kept, lo : lo + 128]
+                        im = spec_wide[half, j, at + kept : at + 2 * kept, lo : lo + 128]
+                        a_re, a_im = adjs[2 * n], adjs[2 * n + 1]
+                        term_re = re * a_re + im * a_im
+                        term_im = re * a_im - im * a_re
+                        grad_re = term_re if n == 0 else grad_re + term_re
+                        grad_im = term_im if n == 0 else grad_im + term_im
+                    grads[m, :, lo : lo + 128] = grad_re
+                    grads[m, :, square + lo : square + lo + 128] = grad_im
+            return 0
+
+        lax.fori_loop(0, quads, weight_terms, 0)
+    store_grads = pltpu.make_async_copy(grads, out_spectral, load_sem.at[3])
+    store_grads.start()
+    wait_all(modes_to_cells(3, 3, back_copies))
+    receive_volume(3, False)
+
+    def finish(step, _):
+        at = columns(step)
+        grad = dot(volume[...], synthesis[:, at]) + dot(mix_back[...], delta[:, at])
+        for u in range(lines):
+            natural[pl.ds(step * lines + u, cell_rows, stride=span_y), :] = grad[
+                :, u * width : (u + 1) * width
+            ]
         return 0
 
-    lax.fori_loop(0, tiles, pull, 0)
-    copies = start_dp(3)
-
-    def weight_terms(m, _):
-        adjs = [adj_wide[m, r * kept : (r + 1) * kept] for r in range(2 * owners)]
-        for s in range(channels * channels // 128):
-            lo = s * 128
-            grad_re, grad_im = None, None
-            for n in range(owners):
-                re = spec_wide[m, 2 * n * kept : (2 * n + 1) * kept, lo : lo + 128]
-                im = spec_wide[m, (2 * n + 1) * kept : (2 * n + 2) * kept, lo : lo + 128]
-                a_re, a_im = adjs[2 * n], adjs[2 * n + 1]
-                term_re = re * a_re + im * a_im
-                term_im = re * a_im - im * a_re
-                grad_re = term_re if n == 0 else grad_re + term_re
-                grad_im = term_im if n == 0 else grad_im + term_im
-            out_spectral[m, :, lo : lo + 128] = grad_re
-            lo2 = channels * channels + lo
-            out_spectral[m, :, lo2 : lo2 + 128] = grad_im
+    lax.fori_loop(0, chunks, finish, 0)
+
+    def narrow(step, _):
+        at = pl.ds(pl.multiple_of(step * 512, 512), 512)
+        out_input[at, :] = natural[at, :].astype(bf16)
         return 0
 
-    lax.fori_loop(0, tiles * quads, weight_terms, 0)
-    wait_all(copies)
-    wait_all(modes_to_cells(3, 3))
-    receive_volume(3, False)
-
-    def finish(step, _):
-        at = pl.ds(pl.multiple_of(step * chunk, chunk), chunk)
-        grad = dot(volume[...], plane[:, at]) + dot(mix_back[...], delta[:, at])
-        out_input[:, at] = grad.astype(bf16)
-        return 0
-
-    lax.fori_loop(0, chunks, finish, 0)
+    lax.fori_loop(0, natural.shape[0] // 512, narrow, 0)
+    store_grads.wait()
 
 
 def fits(features, spectral, owners):
-    samples, channels, slab = features.shape[:3]
+    samples, channels, slab, span_y, span_z = features.shape
     modes, kept = spectral.shape[:2]
     return (
-        samples == 1 and kept == 8 and channels == 32 and slab == 4
-        and modes == 32 and (2 * kept * owners) % 16 == 0
+        samples == 1 and kept == 8 and channels == 32 and slab == 4 and modes == 32
+        and span_z == 128 and span_y % 8 == 0 and (2 * kept * owners) % 16 == 0
     )
 
 
@@ -488,49 +608,69 @@
     tiles = 8
     quads = modes // tiles
     lanes = quads * channels
+    square = channels * channels
     cell_rows, cells_count = channels * slab, span_y * span_z
+    natural_shape = (cell_rows * span_y, span_z)
     plane, doubling = np_plane_rows(span_y, span_z, blocks, tiles, quads)
     line = np_line(slab * blocks, blocks, owners)
-    regroup, spread, tile = np_selectors(channels, slab, quads)
-    eye = jnp.eye(slab, dtype=bf16)
-    mix_back = jnp.einsum("io,xy->ixoy", pointwise, eye).reshape(cell_rows, cell_rows)
-    mix_fwd = jnp.einsum("io,xy->oxiy", pointwise, eye).reshape(cell_rows, cell_rows)
-    bias = jnp.repeat(biases.astype(f32), slab)[:, None]
+    selectors = np_selectors(channels, slab, quads)
     plane_rows = plane.shape[0]
-    sizes = (blocks, owners, channels, slab, tiles, quads, kept)
+    chunks = 8
+    rows = 2 * kept * owners
+    half_rows = rows * tiles // HALVES
+    sizes = (blocks, owners, channels, slab, span_y, tiles, quads, kept)
     vmem = pl.BlockSpec(memory_space=pltpu.VMEM)
+    hbm = pl.BlockSpec(memory_space=pl.ANY)
+    space_shape = (4, blocks, 2 * slab * tiles, lanes)
+    dp_shape = (4 * HALVES, owners, 2 * kept, tiles // HALVES * lanes)
     grad_input, grad_spectral = pl.pallas_call(
         functools.partial(layer_kernel, sizes),
         out_shape=(
-            jax.ShapeDtypeStruct((cell_rows, cells_count), bf16),
+            jax.ShapeDtypeStruct(natural_shape, bf16),
             jax.ShapeDtypeStruct(spectral.shape, f32),
         ),
-        in_specs=[vmem] * 12,
-        out_specs=(vmem, vmem),
+        in_specs=[vmem, hbm, hbm, vmem, vmem, hbm, hbm] + [vmem] * 8,
+        out_specs=(vmem, hbm),
         scratch_shapes=[
-            pltpu.VMEM((plane_rows, cell_rows), f32),
+            pltpu.VMEM(natural_shape, bf16),
+            pltpu.VMEM(spectral.shape, bf16),
+            pltpu.VMEM((cells_count, plane_rows), bf16),
+            pltpu.VMEM((plane_rows, cells_count), bf16),
+            pltpu.VMEM(spectral.shape, f32),
+            pltpu.VMEM(natural_shape, f32),
             pltpu.VMEM((cell_rows, cells_count), bf16),
-            pltpu.VMEM((modes, 2 * kept * owners, channels * channels), f32),
-            pltpu.VMEM((modes, 2 * kept * owners, 128), f32),
-            pltpu.VMEM((blocks * 2 * slab * 8, lanes), f32),
+            pltpu.VMEM((cell_rows, cells_count), bf16),
+            pltpu.VMEM((cell_rows, plane_rows), f32),
             pltpu.VMEM((cell_rows, plane_rows), bf16),
-            pltpu.VMEM((4, blocks, 2 * slab * 8, lanes), bf16),
-            pltpu.VMEM((4, blocks, 2 * slab * 8, lanes), bf16),
-            pltpu.VMEM((4, owners, 2 * kept, modes * channels), bf16),
-            pltpu.VMEM((4, owners, 2 * kept, modes * channels), bf16),
+            pltpu.VMEM((cell_rows, cell_rows), bf16),
+            pltpu.VMEM((cell_rows, cell_rows), bf16),
+            pltpu.VMEM((cell_rows, 1), f32),
+            pltpu.VMEM((half_rows, lanes), bf16),
+            pltpu.VMEM((quads, half_rows, lanes), bf16),
+            pltpu.VMEM((HALVES, quads, half_rows, square), f32),
+            pltpu.VMEM((HALVES, quads, half_rows, lanes), f32),
+            pltpu.VMEM((half_rows, square), bf16),
+            pltpu.VMEM((half_rows, lanes), f32),
+            pltpu.VMEM((blocks * 2 * slab * tiles, lanes), f32),
+            pltpu.VMEM(space_shape, bf16),
+            pltpu.VMEM(space_shape, bf16),
+            pltpu.VMEM(dp_shape, bf16),
+            pltpu.VMEM(dp_shape, bf16),
+            pltpu.SemaphoreType.DMA((4,)),
+            pltpu.SemaphoreType.DMA((chunks,)),
             pltpu.SemaphoreType.DMA((4, blocks)),
             pltpu.SemaphoreType.DMA((4, blocks)),
-            pltpu.SemaphoreType.DMA((4, owners)),
-            pltpu.SemaphoreType.DMA((4, owners)),
+            pltpu.SemaphoreType.DMA((4 * HALVES, owners)),
+            pltpu.SemaphoreType.DMA((4 * HALVES, owners)),
         ],
         compiler_params=pltpu.CompilerParams(
             collective_id=0, has_side_effects=True, vmem_limit_bytes=56 * 1024 * 1024
         ),
     )(
-        features.reshape(cell_rows, cells_count),
-        cotangent.reshape(cell_rows, cells_count),
-        spectral, mix_fwd, mix_back, bias,
-        plane, doubling, line, regroup, spread, tile,
+        features.reshape(natural_shape),
+        cotangent.reshape(natural_shape),
+        spectral, pointwise, biases[None, :],
+        np.ascontiguousarray(plane.T), plane, doubling.T, line, *selectors,
     )
     return grad_input.reshape(features.shape), grad_spectral
 

time: 82.3 us -> 62.5 us (0.76)
  Pallas kernels: 65.9 us -> 56.2 us
  local copies, waits for them, and re-layouts: 14.6 us -> 5.44 us
  other arithmetic: 0.91 us -> 0 us
    pallas_call x1, Pallas kernels: 65.9 us -> 56.2 us  [body(): pl.pallas_call(functools.partial(layer_kernel, sizes), out_shape=(jax.Sha...]
    reshape x3 -> x0, local copies, waits for them, and re-layouts: 8.58 us -> none  [the longest x1 3.47 us: body(): cotangent.reshape(cell_rows, cells_count)]
    unnamed x6 -> x2, local copies, waits for them, and re-layouts: 3.9 us -> 5.44 us
    transpose x1 -> x0, other arithmetic: 0.9 us -> none  [body(): jnp.einsum('io,xy->ixoy', pointwise, eye).reshape(cell_rows, cell_rows)]
where the time goes in v1:
time: 62.5 us; the launch traced here: 62.3 us
  Pallas kernels  56.2 us (90%)
  local copies, waits for them, and re-layouts  5.44 us (9%)
  between operations  0.64 us (1%)
    pallas_call x1, Pallas kernels, body(): pl.pallas_call(functools.partial(layer_kernel, sizes), out_shape=(jax.Sha...  56.2 us
    unnamed x2, local copies, waits for them, and re-layouts  5.44 us

profile of v1, /device:TPU:0, one launch (start us, length us, event | category | flops | bytes accessed | tf_op | source)
XLA Modules:
  0.0 62.3 jit_solution(11357874680569822862)
XLA Ops:
  0.6 56.2 %shard_map.158 = (bf16[4096,128]{1,0:T(8,128)(2,1)}, f32[32,8,2048]{2,1,0:T(8,128)}) custom-call(bf16[4096,128]{1,0:T(8,128)(2,1)} %bitcast.4, bf16[4096,128]{1,0:T(8,128)(2,1)} %bitcast.5, bf16[32,8,2048]{2,1,0:T(8,128)(2,1)} %weights_hbm.1, bf16[32,32]{1,0:T(8,128)(2,1)} %pointwise.1, bf16[1,32]{1,0:T(2,128)(2,1)} %bitcast.7, ...), custom_call_target="tpu_custom_call" | custom-call | tf_op jit(solution)/shard_map/pallas_call | solution.py:626
  56.9 2.3 %copy.19 = bf16[1,32,4,32,128]{4,3,2,1,0:T(8,128)(2,1)} copy(bf16[1,32,4,32,128]{4,3,2,1,0:T(8,128)(2,1)} %bitcast.6) | data formatting | bytes 2097152
  59.2 3.1 %copy.20 = f32[32,8,2048]{2,1,0:T(8,128)} copy(f32[32,8,2048]{2,1,0:T(8,128)} %get-tuple-element.9) | data formatting | bytes 4194304

commit v2 on v1

--- a/solution.py
+++ b/solution.py
@@ -169,6 +169,9 @@
     return (grad_input, grad_spectral)
 
 
+HALVES = 2
+
+
 def np_frequencies(kept_count, length):
     indices = np.arange(kept_count)
     return np.where(indices < kept_count // 2, indices, indices + (length - kept_count))
@@ -182,10 +185,12 @@
     )
     factor = 1.0 / math.sqrt(count_y * count_z)
     table = np.stack([factor * np.cos(angles), -factor * np.sin(angles)], axis=0)
-    table = table.reshape(2, count_y * count_z, blocks, tiles, quads)
-    rows = table.transpose(4, 2, 0, 3, 1).reshape(-1, count_y * count_z)
-    doubling = np.where(np.arange(KY * KZ) % KZ == 0, 1.0, 2.0).reshape(blocks, 1, tiles, quads)
-    doubling = np.broadcast_to(doubling, (blocks, 2, tiles, quads)).transpose(3, 0, 1, 2)
+    near = tiles // HALVES
+    table = table.reshape(2, count_y * count_z, blocks, HALVES, near, quads)
+    rows = table.transpose(5, 2, 3, 0, 4, 1).reshape(-1, count_y * count_z)
+    doubling = np.where(np.arange(KY * KZ) % KZ == 0, 1.0, 2.0)
+    doubling = doubling.reshape(blocks, HALVES, 1, near, quads)
+    doubling = np.broadcast_to(doubling, (blocks, HALVES, 2, near, quads)).transpose(4, 0, 1, 2, 3)
     return rows.astype(ml_dtypes.bfloat16), doubling.reshape(-1, 1).astype(np.float32)
 
 
@@ -198,7 +203,7 @@
         [np.stack([cos_part, -sine_part], 0), np.stack([sine_part, cos_part], 0)], 0
     )
     table = table.reshape(2, 2, blocks, full_length // blocks, owners, KX // owners)
-    table = table.transpose(4, 1, 5, 2, 0, 3).reshape(2 * KX, 2 * full_length)
+    table = table.transpose(4, 1, 5, 2, 3, 0).reshape(2 * KX, 2 * full_length)
     return table.astype(ml_dtypes.bfloat16)
 
 
@@ -234,7 +239,6 @@
 f32, bf16 = jnp.float32, jnp.bfloat16
 NT = (((1,), (1,)), ((), ()))
 TN = (((0,), (0,)), ((), ()))
-HALVES = 2
 
 
 def dot(left, right):
@@ -272,10 +276,10 @@
 def layer_kernel(
     sizes,
     feats, cot_hbm, weights_hbm, pointwise, biases, analysis_hbm, synthesis_hbm,
-    doubling, line, regroup, spread, gather, tile, untile, repeat,
-    out_input, out_spectral,
-    cot, weights, analysis, synthesis, grads,
-    natural, rows_in, delta, coarse_acc, volume, mix_fwd, mix_back, bias,
+    regroup_hbm, spread_hbm, gather_hbm, tile_hbm, untile_hbm, repeat, doubling, line,
+    out_cells, out_delta, out_grads, mix_back,
+    cot, weights, analysis, synthesis, regroup, spread, gather, tile, untile, grads,
+    natural, rows_in, delta, coarse_acc, volume, mix_fwd, bias,
     stack, parts, spec_wide, adj_wide, products, pulled, cells,
     space_send, space_recv, dp_send, dp_recv,
     load_sem, analysis_sem, space_ssem, space_rsem, dp_ssem, dp_rsem,
@@ -307,8 +311,18 @@
     load_cot = pltpu.make_async_copy(cot_hbm, cot, load_sem.at[0])
     load_weights = pltpu.make_async_copy(weights_hbm, weights, load_sem.at[1])
     load_synthesis = pltpu.make_async_copy(synthesis_hbm, synthesis, load_sem.at[2])
+    load_tables = [
+        pltpu.make_async_copy(source, target, load_sem.at[5 + at])
+        for at, (source, target) in enumerate(
+            [(regroup_hbm, regroup), (spread_hbm, spread), (tile_hbm, tile),
+             (untile_hbm, untile), (gather_hbm, gather)]
+        )
+    ]
+    load_tables[0].start()
     load_cot.start()
     load_weights.start()
+    for copy in load_tables[1:]:
+        copy.start()
     load_synthesis.start()
 
     barrier = pltpu.get_barrier_semaphore()
@@ -336,10 +350,11 @@
     def columns(step):
         return pl.ds(pl.multiple_of(step * chunk, chunk), chunk)
 
-    def send_space(turn):
+    def send_space(turn, half):
+        at = turn * HALVES + half
         return start_exchange(
-            "space", blocks, space_send.at[turn], space_recv.at[turn],
-            space_ssem.at[turn], space_rsem.at[turn],
+            "space", blocks, space_send.at[at], space_recv.at[at],
+            space_ssem.at[at], space_rsem.at[at],
         )
 
     def send_dp(turn, half):
@@ -353,27 +368,26 @@
             [coarse[:, j * group : (j + 1) * group].T.astype(bf16) for j in range(quads)], axis=1
         )
         wide = dot(wide, regroup[...])
-        for block in range(blocks):
-            pieces = [
-                wide[
-                    (block * 2 + p) * tiles : (block * 2 + p + 1) * tiles,
-                    x * lanes : (x + 1) * lanes,
-                ]
-                for p in range(2)
-                for x in range(slab)
-            ]
-            space_send[turn, block] = jnp.concatenate(pieces, axis=0).astype(bf16)
-        return send_space(turn)
-
-    def cells_to_modes(turn, dp_turn):
-        cells[...] = space_recv[turn].astype(f32).reshape(cells.shape)
         copies = []
         for half in range(HALVES):
+            for block in range(blocks):
+                at = (block * HALVES + half) * 2 * near
+                pieces = [
+                    wide[at : at + 2 * near, x * lanes : (x + 1) * lanes] for x in range(slab)
+                ]
+                space_send[turn * HALVES + half, block] = jnp.concatenate(pieces, axis=0).astype(
+                    bf16
+                )
+            copies.append(send_space(turn, half))
+        return copies
+
+    def cells_to_modes(turn, dp_turn, arriving):
+        copies = []
+        for half in range(HALVES):
+            wait_all(arriving[half])
+            cells[half] = space_recv[turn * HALVES + half].astype(f32).reshape(cells.shape[1:])
             wide = jnp.concatenate(
-                [
-                    cells[pl.ds(half * near + t, blocks * 2 * slab, stride=tiles), :]
-                    for t in range(near)
-                ],
+                [cells[half, pl.ds(t, blocks * 2 * slab, stride=near), :] for t in range(near)],
                 axis=1,
             ).astype(bf16)
             spectrum = dot(line[...], wide).astype(bf16)
@@ -381,38 +395,21 @@
             copies.append(send_dp(dp_turn, half))
         return copies
 
-    def modes_to_cells(dp_turn, turn, copies):
+    def modes_to_cells(dp_turn, turn, arriving):
+        copies = []
         for half in range(HALVES):
-            wait_all(copies[half])
+            wait_all(arriving[half])
             wide = dp_recv[dp_turn * HALVES + half].reshape(rows, near * lanes)
             back = lax.dot_general(line[...], wide, TN, preferred_element_type=f32)
             for t in range(near):
-                cells[pl.ds(half * near + t, blocks * 2 * slab, stride=tiles), :] = back[
+                cells[half, pl.ds(t, blocks * 2 * slab, stride=near), :] = back[
                     :, t * lanes : (t + 1) * lanes
                 ]
-        space_send[turn] = cells[...].astype(bf16).reshape(space_send.shape[1:])
-        return send_space(turn)
-
-    def receive_volume(turn, scaled):
-        pieces = []
-        for block in range(blocks):
-            held = space_recv[turn, block].astype(f32)
-            for p in range(2):
-                pieces.append(
-                    jnp.concatenate(
-                        [
-                            held[(p * slab + x) * tiles : (p * slab + x + 1) * tiles]
-                            for x in range(slab)
-                        ],
-                        axis=1,
-                    )
-                )
-        wide = dot_nt(jnp.concatenate(pieces, axis=0).astype(bf16), regroup[...])
-        for j in range(quads):
-            part = wide[:, j * lanes : (j + 1) * lanes].T
-            if scaled:
-                part = part * doubling[:, j * group : (j + 1) * group]
-            volume[:, j * group : (j + 1) * group] = part.astype(bf16)
+            space_send[turn * HALVES + half] = (
+                cells[half].astype(bf16).reshape(space_send.shape[1:])
+            )
+            copies.append(send_space(turn, half))
+        return copies
 
     def stack_half(dp_turn, half):
         for t in range(near):
@@ -442,6 +439,7 @@
         rows_in[:, step * chunk : (step + 1) * chunk] = part
         coarse_acc[...] += dot(part, analysis[step * chunk : (step + 1) * chunk, :])
     pl.semaphore_wait(barrier, blocks + owners - 2)
+    load_tables[0].wait()
     copies = send_cells(0, coarse_acc[...])
 
     same_cell = lax.rem(lax.broadcasted_iota(jnp.int32, mix_fwd.shape, 0), slab) == lax.rem(
@@ -456,9 +454,10 @@
     )
     load_cot.wait()
     widen(cot)
-    wait_all(copies)
-    copies = cells_to_modes(0, 0)
+    copies = cells_to_modes(0, 0, copies)
     load_weights.wait()
+    for copy in load_tables[1:]:
+        copy.wait()
 
     back_copies = []
     for half in range(HALVES):
@@ -488,9 +487,13 @@
         lax.fori_loop(0, quads, mix, 0)
         mixed = dot(jnp.concatenate([parts[j] for j in range(quads)], axis=1), tile[...])
         back_copies.append(unstack_half(1, half, mixed))
-    wait_all(modes_to_cells(1, 1, back_copies))
+    copies = modes_to_cells(1, 1, back_copies)
     load_synthesis.wait()
-    receive_volume(1, True)
+    for half in range(HALVES):
+        wait_all(copies[half])
+    collect_volume(
+        slab, space_recv.at[pl.ds(HALVES, HALVES)], regroup, volume, doubling
+    )
 
     coarse_acc[...] = jnp.zeros_like(coarse_acc)
 
@@ -503,8 +506,10 @@
         return 0
 
     lax.fori_loop(0, chunks, activate, 0)
-    wait_all(send_cells(2, coarse_acc[...] * doubling[...]))
-    copies = cells_to_modes(2, 2)
+    copies = send_cells(2, coarse_acc[...] * doubling[...])
+    store_delta = pltpu.make_async_copy(delta, out_delta, load_sem.at[4])
+    store_delta.start()
+    copies = cells_to_modes(2, 2, copies)
 
     back_copies = []
     for half in range(HALVES):
@@ -565,21 +570,72 @@
             return 0
 
         lax.fori_loop(0, quads, weight_terms, 0)
-    store_grads = pltpu.make_async_copy(grads, out_spectral, load_sem.at[3])
+    store_grads = pltpu.make_async_copy(grads, out_grads, load_sem.at[3])
     store_grads.start()
-    wait_all(modes_to_cells(3, 3, back_copies))
-    receive_volume(3, False)
-
-    def finish(step, _):
-        at = columns(step)
+    copies = modes_to_cells(3, 3, back_copies)
+    for half in range(HALVES):
+        wait_all(copies[half])
+        out_cells[half] = space_recv[3 * HALVES + half]
+    store_delta.wait()
+    store_grads.wait()
+
+
+def collect_volume(slab, arrived, regroup, volume, doubling):
+    pieces = []
+    lanes = arrived.shape[3]
+    tile_rows = arrived.shape[2] // slab
+    group = arrived.shape[1] * HALVES * tile_rows
+    for block in range(arrived.shape[1]):
+        for half in range(HALVES):
+            held = arrived[half, block].astype(f32)
+            pieces.append(
+                jnp.concatenate(
+                    [held[x * tile_rows : (x + 1) * tile_rows] for x in range(slab)], axis=1
+                )
+            )
+    wide = dot_nt(jnp.concatenate(pieces, axis=0).astype(bf16), regroup[...])
+    for j in range(wide.shape[1] // lanes):
+        part = wide[:, j * lanes : (j + 1) * lanes].T
+        if doubling is not None:
+            part = part * doubling[:, j * group : (j + 1) * group]
+        volume[:, j * group : (j + 1) * group] = part.astype(bf16)
+
+
+def result_kernel(
+    slab, arrived, mix_back, regroup, delta_hbm, grads_hbm, synthesis_hbm,
+    out_input, out_spectral,
+    delta, synthesis, volume, natural, sems, synthesis_sem,
+):
+    cell_rows, cells_count = delta.shape
+    chunks = synthesis_sem.shape[0]
+    chunk = cells_count // chunks
+    width = natural.shape[1]
+    lines = chunk // width
+    span_y = cells_count // width
+    load_delta = pltpu.make_async_copy(delta_hbm, delta, sems.at[0])
+    load_delta.start()
+    loads = [
+        pltpu.make_async_copy(
+            synthesis_hbm.at[:, pl.ds(step * chunk, chunk)],
+            synthesis.at[:, pl.ds(step * chunk, chunk)],
+            synthesis_sem.at[step],
+        )
+        for step in range(chunks)
+    ]
+    for copy in loads:
+        copy.start()
+    pass_grads = pltpu.make_async_copy(grads_hbm, out_spectral, sems.at[1])
+    pass_grads.start()
+    collect_volume(slab, arrived, regroup, volume, None)
+    load_delta.wait()
+    for step in range(chunks):
+        loads[step].wait()
+        at = slice(step * chunk, (step + 1) * chunk)
         grad = dot(volume[...], synthesis[:, at]) + dot(mix_back[...], delta[:, at])
         for u in range(lines):
             natural[pl.ds(step * lines + u, cell_rows, stride=span_y), :] = grad[
                 :, u * width : (u + 1) * width
             ]
-        return 0
-
-    lax.fori_loop(0, chunks, finish, 0)
 
     def narrow(step, _):
         at = pl.ds(pl.multiple_of(step * 512, 512), 512)
@@ -587,7 +643,7 @@
         return 0
 
     lax.fori_loop(0, natural.shape[0] // 512, narrow, 0)
-    store_grads.wait()
+    pass_grads.wait()
 
 
 def fits(features, spectral, owners):
@@ -613,7 +669,6 @@
     natural_shape = (cell_rows * span_y, span_z)
     plane, doubling = np_plane_rows(span_y, span_z, blocks, tiles, quads)
     line = np_line(slab * blocks, blocks, owners)
-    selectors = np_selectors(channels, slab, quads)
     plane_rows = plane.shape[0]
     chunks = 8
     rows = 2 * kept * owners
@@ -621,28 +676,35 @@
     sizes = (blocks, owners, channels, slab, span_y, tiles, quads, kept)
     vmem = pl.BlockSpec(memory_space=pltpu.VMEM)
     hbm = pl.BlockSpec(memory_space=pl.ANY)
-    space_shape = (4, blocks, 2 * slab * tiles, lanes)
+    space_shape = (4 * HALVES, blocks, 2 * slab * tiles // HALVES, lanes)
     dp_shape = (4 * HALVES, owners, 2 * kept, tiles // HALVES * lanes)
-    grad_input, grad_spectral = pl.pallas_call(
+    regroup, spread, gather, tile, untile, repeat = np_selectors(channels, slab, quads)
+    arrived, delta, grads, mix_back = pl.pallas_call(
         functools.partial(layer_kernel, sizes),
         out_shape=(
-            jax.ShapeDtypeStruct(natural_shape, bf16),
+            jax.ShapeDtypeStruct((HALVES,) + space_shape[1:], bf16),
+            jax.ShapeDtypeStruct((cell_rows, cells_count), bf16),
             jax.ShapeDtypeStruct(spectral.shape, f32),
+            jax.ShapeDtypeStruct((cell_rows, cell_rows), bf16),
         ),
-        in_specs=[vmem, hbm, hbm, vmem, vmem, hbm, hbm] + [vmem] * 8,
-        out_specs=(vmem, hbm),
+        in_specs=[vmem, hbm, hbm, vmem, vmem] + [hbm] * 7 + [vmem] * 3,
+        out_specs=(vmem, hbm, hbm, vmem),
         scratch_shapes=[
             pltpu.VMEM(natural_shape, bf16),
             pltpu.VMEM(spectral.shape, bf16),
             pltpu.VMEM((cells_count, plane_rows), bf16),
             pltpu.VMEM((plane_rows, cells_count), bf16),
+            pltpu.VMEM(regroup.shape, bf16),
+            pltpu.VMEM(spread.shape, bf16),
+            pltpu.VMEM(gather.shape, bf16),
+            pltpu.VMEM(tile.shape, bf16),
+            pltpu.VMEM(untile.shape, bf16),
             pltpu.VMEM(spectral.shape, f32),
             pltpu.VMEM(natural_shape, f32),
             pltpu.VMEM((cell_rows, cells_count), bf16),
             pltpu.VMEM((cell_rows, cells_count), bf16),
             pltpu.VMEM((cell_rows, plane_rows), f32),
             pltpu.VMEM((cell_rows, plane_rows), bf16),
-            pltpu.VMEM((cell_rows, cell_rows), bf16),
             pltpu.VMEM((cell_rows, cell_rows), bf16),
             pltpu.VMEM((cell_rows, 1), f32),
             pltpu.VMEM((half_rows, lanes), bf16),
@@ -651,15 +713,15 @@
             pltpu.VMEM((HALVES, quads, half_rows, lanes), f32),
             pltpu.VMEM((half_rows, square), bf16),
             pltpu.VMEM((half_rows, lanes), f32),
-            pltpu.VMEM((blocks * 2 * slab * tiles, lanes), f32),
+            pltpu.VMEM((HALVES, blocks * 2 * slab * tiles // HALVES, lanes), f32),
             pltpu.VMEM(space_shape, bf16),
             pltpu.VMEM(space_shape, bf16),
             pltpu.VMEM(dp_shape, bf16),
             pltpu.VMEM(dp_shape, bf16),
-            pltpu.SemaphoreType.DMA((4,)),
+            pltpu.SemaphoreType.DMA((10,)),
             pltpu.SemaphoreType.DMA((chunks,)),
-            pltpu.SemaphoreType.DMA((4, blocks)),
-            pltpu.SemaphoreType.DMA((4, blocks)),
+            pltpu.SemaphoreType.DMA((4 * HALVES, blocks)),
+            pltpu.SemaphoreType.DMA((4 * HALVES, blocks)),
             pltpu.SemaphoreType.DMA((4 * HALVES, owners)),
             pltpu.SemaphoreType.DMA((4 * HALVES, owners)),
         ],
@@ -670,8 +732,27 @@
         features.reshape(natural_shape),
         cotangent.reshape(natural_shape),
         spectral, pointwise, biases[None, :],
-        np.ascontiguousarray(plane.T), plane, doubling.T, line, *selectors,
-    )
+        np.ascontiguousarray(plane.T), plane,
+        regroup, spread, gather, tile, untile, repeat, doubling.T, line,
+    )
+    grad_input, grad_spectral = pl.pallas_call(
+        functools.partial(result_kernel, slab),
+        out_shape=(
+            jax.ShapeDtypeStruct(natural_shape, bf16),
+            jax.ShapeDtypeStruct(spectral.shape, f32),
+        ),
+        in_specs=[vmem, vmem, vmem, hbm, hbm, hbm],
+        out_specs=(vmem, hbm),
+        scratch_shapes=[
+            pltpu.VMEM((cell_rows, cells_count), bf16),
+            pltpu.VMEM((plane_rows, cells_count), bf16),
+            pltpu.VMEM((cell_rows, plane_rows), bf16),
+            pltpu.VMEM(natural_shape, f32),
+            pltpu.SemaphoreType.DMA((2,)),
+            pltpu.SemaphoreType.DMA((chunks,)),
+        ],
+        compiler_params=pltpu.CompilerParams(vmem_limit_bytes=56 * 1024 * 1024),
+    )(arrived, mix_back, regroup, delta, grads, plane)
     return grad_input.reshape(features.shape), grad_spectral
 
 

time: 62.5 us -> 120 us (1.92)
  Pallas kernels: 56.2 us -> 119 us
  local copies, waits for them, and re-layouts: 5.44 us -> 0 us
    pallas_call x0 -> x1, Pallas kernels: none -> 66.8 us  [body(): pl.pallas_call(functools.partial(result_kernel, slab), out_shape=(jax.Sha...]
    unnamed x2 -> x0, local copies, waits for them, and re-layouts: 5.44 us -> none
    pallas_call x1, Pallas kernels: 56.2 us -> 52.1 us  [body(): pl.pallas_call(functools.partial(layer_kernel, sizes), out_shape=(jax.Sha...]
where the time goes in v2:
time: 120 us
  Pallas kernels  119 us (99%)
    pallas_call x1, Pallas kernels, body(): pl.pallas_call(functools.partial(result_kernel, slab), out_shape=(jax.Sha...  66.8 us
    pallas_call x1, Pallas kernels, body(): pl.pallas_call(functools.partial(layer_kernel, sizes), out_shape=(jax.Sha...  52.1 us

profile of v2, /device:TPU:0, one launch (start us, length us, event | category | flops | bytes accessed | tf_op | source)
XLA Modules:
  0.0 119.6 jit_solution(7603577969664973863)
XLA Ops:
  0.6 52.1 %shard_map.158 = (bf16[2,8,32,128]{3,2,1,0:T(8,128)(2,1)}, bf16[128,4096]{1,0:T(8,128)(2,1)}, f32[32,8,2048]{2,1,0:T(8,128)}, bf16[128,128]{1,0:T(8,128)(2,1)}) custom-call(bf16[4096,128]{1,0:T(8,128)(2,1)} %bitcast.4, bf16[4096,128]{1,0:T(8,128)(2,1)} %bitcast.5, bf16[32,8,2048]{2,1,0:T(8,128)(2,1)} %weights_hbm.1, bf16[32,32]{1,0:T(8,128)(2,1)} %pointwise.1, ...), custom_call_target="tpu_custom_call" | custom-call | tf_op jit(solution)/shard_map/pallas_call | solution.py:682
  52.8 66.8 %shard_map.159 = (bf16[4096,128]{1,0:T(8,128)(2,1)}, f32[32,8,2048]{2,1,0:T(8,128)}) custom-call(bf16[2,8,32,128]{3,2,1,0:T(8,128)(2,1)} %get-tuple-element.8.arrived, bf16[128,128]{1,0:T(8,128)(2,1)} %get-tuple-element.9.mix_back, bf16[512,512]{1,0:T(8,128)(2,1)} %constant.22.clone.regroup_hbm.regroup, bf16[128,4096]{1,0:T(8,128)(2,1)} %get-tuple-element.10.delta_hbm, ...), custom_call_target="tpu_custom_call" | custom-call | tf_op jit(solution)/shard_map/pallas_call | solution.py:738

commit v3 on v2

--- a/solution.py
+++ b/solution.py
@@ -187,10 +187,10 @@
     table = np.stack([factor * np.cos(angles), -factor * np.sin(angles)], axis=0)
     near = tiles // HALVES
     table = table.reshape(2, count_y * count_z, blocks, HALVES, near, quads)
-    rows = table.transpose(5, 2, 3, 0, 4, 1).reshape(-1, count_y * count_z)
+    rows = table.transpose(3, 5, 2, 0, 4, 1).reshape(-1, count_y * count_z)
     doubling = np.where(np.arange(KY * KZ) % KZ == 0, 1.0, 2.0)
     doubling = doubling.reshape(blocks, HALVES, 1, near, quads)
-    doubling = np.broadcast_to(doubling, (blocks, HALVES, 2, near, quads)).transpose(4, 0, 1, 2, 3)
+    doubling = np.broadcast_to(doubling, (blocks, HALVES, 2, near, quads)).transpose(1, 4, 0, 2, 3)
     return rows.astype(ml_dtypes.bfloat16), doubling.reshape(-1, 1).astype(np.float32)
 
 
@@ -279,7 +279,7 @@
     regroup_hbm, spread_hbm, gather_hbm, tile_hbm, untile_hbm, repeat, doubling, line,
     out_cells, out_delta, out_grads, mix_back,
     cot, weights, analysis, synthesis, regroup, spread, gather, tile, untile, grads,
-    natural, rows_in, delta, coarse_acc, volume, mix_fwd, bias,
+    natural, rows_in, linear, upstream, delta, coarse_acc, volume, mix_fwd, bias,
     stack, parts, spec_wide, adj_wide, products, pulled, cells,
     space_send, space_recv, dp_send, dp_recv,
     load_sem, analysis_sem, space_ssem, space_rsem, dp_ssem, dp_rsem,
@@ -293,8 +293,9 @@
     chunk = analysis_hbm.shape[0] // analysis_sem.shape[0]
     chunks = cells_count // chunk
     lines = chunk // width
-    group = blocks * 2 * tiles
     near = tiles // HALVES
+    group = blocks * 2 * near
+    part_columns = quads * group
     square = channels * channels
     mesh_id = pl.DeviceIdType.MESH
 
@@ -363,23 +364,16 @@
             "dp", owners, dp_send.at[at], dp_recv.at[at], dp_ssem.at[at], dp_rsem.at[at]
         )
 
-    def send_cells(turn, coarse):
+    def send_cells(turn, half, coarse):
         wide = jnp.concatenate(
             [coarse[:, j * group : (j + 1) * group].T.astype(bf16) for j in range(quads)], axis=1
         )
         wide = dot(wide, regroup[...])
-        copies = []
-        for half in range(HALVES):
-            for block in range(blocks):
-                at = (block * HALVES + half) * 2 * near
-                pieces = [
-                    wide[at : at + 2 * near, x * lanes : (x + 1) * lanes] for x in range(slab)
-                ]
-                space_send[turn * HALVES + half, block] = jnp.concatenate(pieces, axis=0).astype(
-                    bf16
-                )
-            copies.append(send_space(turn, half))
-        return copies
+        for block in range(blocks):
+            at = block * 2 * near
+            pieces = [wide[at : at + 2 * near, x * lanes : (x + 1) * lanes] for x in range(slab)]
+            space_send[turn * HALVES + half, block] = jnp.concatenate(pieces, axis=0).astype(bf16)
+        return send_space(turn, half)
 
     def cells_to_modes(turn, dp_turn, arriving):
         copies = []
@@ -432,15 +426,25 @@
         )
 
     widen(feats)
-    coarse_acc[...] = jnp.zeros_like(coarse_acc)
     for step in range(chunks):
-        analysis_loads[step].wait()
-        part = plane_lines(step).astype(bf16)
-        rows_in[:, step * chunk : (step + 1) * chunk] = part
-        coarse_acc[...] += dot(part, analysis[step * chunk : (step + 1) * chunk, :])
+        rows_in[:, step * chunk : (step + 1) * chunk] = plane_lines(step).astype(bf16)
+
+    def analyse(half, source):
+        at = slice(half * part_columns, (half + 1) * part_columns)
+        coarse_acc[...] = jnp.zeros_like(coarse_acc)
+        for step in range(chunks):
+            if half == 0 and source is rows_in:
+                analysis_loads[step].wait()
+            rows_at = slice(step * chunk, (step + 1) * chunk)
+            coarse_acc[...] += dot(source[:, rows_at], analysis[rows_at, at])
+        return coarse_acc[...]
+
+    coarse = analyse(0, rows_in)
     pl.semaphore_wait(barrier, blocks + owners - 2)
     load_tables[0].wait()
-    copies = send_cells(0, coarse_acc[...])
+    copies = [send_cells(0, 0, coarse)]
+    for half in range(1, HALVES):
+        copies.append(send_cells(0, half, analyse(half, rows_in)))
 
     same_cell = lax.rem(lax.broadcasted_iota(jnp.int32, mix_fwd.shape, 0), slab) == lax.rem(
         lax.broadcasted_iota(jnp.int32, mix_fwd.shape, 1), slab
@@ -454,6 +458,14 @@
     )
     load_cot.wait()
     widen(cot)
+
+    def prepare(step, _):
+        at = columns(step)
+        linear[:, at] = dot(mix_fwd[...], rows_in[:, at]) + bias[...]
+        upstream[:, at] = plane_lines(step)
+        return 0
+
+    lax.fori_loop(0, chunks, prepare, 0)
     copies = cells_to_modes(0, 0, copies)
     load_weights.wait()
     for copy in load_tables[1:]:
@@ -491,22 +503,21 @@
     load_synthesis.wait()
     for half in range(HALVES):
         wait_all(copies[half])
-    collect_volume(
-        slab, space_recv.at[pl.ds(HALVES, HALVES)], regroup, volume, doubling
-    )
-
-    coarse_acc[...] = jnp.zeros_like(coarse_acc)
+        collect_volume(
+            slab, half, space_recv.at[HALVES + half], regroup, volume, doubling
+        )
 
     def activate(step, _):
         at = columns(step)
-        pre_act = dot(volume[...], synthesis[:, at]) + dot(mix_fwd[...], rows_in[:, at]) + bias[...]
-        part = (plane_lines(step) * gelu_slope(pre_act)).astype(bf16)
-        delta[:, at] = part
-        coarse_acc[...] += dot(part, analysis[at, :])
+        pre_act = dot(volume[...], synthesis[:, at]) + linear[:, at]
+        delta[:, at] = (upstream[:, at] * gelu_slope(pre_act)).astype(bf16)
         return 0
 
     lax.fori_loop(0, chunks, activate, 0)
-    copies = send_cells(2, coarse_acc[...] * doubling[...])
+    copies = []
+    for half in range(HALVES):
+        at = slice(half * part_columns, (half + 1) * part_columns)
+        copies.append(send_cells(2, half, analyse(half, delta) * doubling[:, at]))
     store_delta = pltpu.make_async_copy(delta, out_delta, load_sem.at[4])
     store_delta.start()
     copies = cells_to_modes(2, 2, copies)
@@ -580,31 +591,32 @@
     store_grads.wait()
 
 
-def collect_volume(slab, arrived, regroup, volume, doubling):
+def collect_volume(slab, half, arrived, regroup, volume, doubling):
+    blocks, lanes = arrived.shape[0], arrived.shape[2]
+    tile_rows = arrived.shape[1] // slab
+    group = blocks * tile_rows
     pieces = []
-    lanes = arrived.shape[3]
-    tile_rows = arrived.shape[2] // slab
-    group = arrived.shape[1] * HALVES * tile_rows
-    for block in range(arrived.shape[1]):
-        for half in range(HALVES):
-            held = arrived[half, block].astype(f32)
-            pieces.append(
-                jnp.concatenate(
-                    [held[x * tile_rows : (x + 1) * tile_rows] for x in range(slab)], axis=1
-                )
+    for block in range(blocks):
+        held = arrived[block].astype(f32)
+        pieces.append(
+            jnp.concatenate(
+                [held[x * tile_rows : (x + 1) * tile_rows] for x in range(slab)], axis=1
             )
+        )
     wide = dot_nt(jnp.concatenate(pieces, axis=0).astype(bf16), regroup[...])
-    for j in range(wide.shape[1] // lanes):
+    quads = wide.shape[1] // lanes
+    for j in range(quads):
+        at = slice((half * quads + j) * group, (half * quads + j + 1) * group)
         part = wide[:, j * lanes : (j + 1) * lanes].T
         if doubling is not None:
-            part = part * doubling[:, j * group : (j + 1) * group]
-        volume[:, j * group : (j + 1) * group] = part.astype(bf16)
+            part = part * doubling[:, at]
+        volume[:, at] = part.astype(bf16)
 
 
 def result_kernel(
     slab, arrived, mix_back, regroup, delta_hbm, grads_hbm, synthesis_hbm,
     out_input, out_spectral,
-    delta, synthesis, volume, natural, sems, synthesis_sem,
+    delta, grads, synthesis, volume, natural, sems, synthesis_sem,
 ):
     cell_rows, cells_count = delta.shape
     chunks = synthesis_sem.shape[0]
@@ -624,9 +636,10 @@
     ]
     for copy in loads:
         copy.start()
-    pass_grads = pltpu.make_async_copy(grads_hbm, out_spectral, sems.at[1])
-    pass_grads.start()
-    collect_volume(slab, arrived, regroup, volume, None)
+    load_grads = pltpu.make_async_copy(grads_hbm, grads, sems.at[1])
+    load_grads.start()
+    for half in range(HALVES):
+        collect_volume(slab, half, arrived.at[half], regroup, volume, None)
     load_delta.wait()
     for step in range(chunks):
         loads[step].wait()
@@ -636,6 +649,9 @@
             natural[pl.ds(step * lines + u, cell_rows, stride=span_y), :] = grad[
                 :, u * width : (u + 1) * width
             ]
+    load_grads.wait()
+    store_grads = pltpu.make_async_copy(grads, out_spectral, sems.at[2])
+    store_grads.start()
 
     def narrow(step, _):
         at = pl.ds(pl.multiple_of(step * 512, 512), 512)
@@ -643,7 +659,7 @@
         return 0
 
     lax.fori_loop(0, natural.shape[0] // 512, narrow, 0)
-    pass_grads.wait()
+    store_grads.wait()
 
 
 def fits(features, spectral, owners):
@@ -702,8 +718,10 @@
             pltpu.VMEM(spectral.shape, f32),
             pltpu.VMEM(natural_shape, f32),
             pltpu.VMEM((cell_rows, cells_count), bf16),
+            pltpu.VMEM((cell_rows, cells_count), f32),
+            pltpu.VMEM((cell_rows, cells_count), f32),
             pltpu.VMEM((cell_rows, cells_count), bf16),
-            pltpu.VMEM((cell_rows, plane_rows), f32),
+            pltpu.VMEM((cell_rows, plane_rows // HALVES), f32),
             pltpu.VMEM((cell_rows, plane_rows), bf16),
             pltpu.VMEM((cell_rows, cell_rows), bf16),
             pltpu.VMEM((cell_rows, 1), f32),
@@ -745,10 +763,11 @@
         out_specs=(vmem, hbm),
         scratch_shapes=[
             pltpu.VMEM((cell_rows, cells_count), bf16),
+            pltpu.VMEM(spectral.shape, f32),
             pltpu.VMEM((plane_rows, cells_count), bf16),
             pltpu.VMEM((cell_rows, plane_rows), bf16),
             pltpu.VMEM(natural_shape, f32),
-            pltpu.SemaphoreType.DMA((2,)),
+            pltpu.SemaphoreType.DMA((3,)),
             pltpu.SemaphoreType.DMA((chunks,)),
         ],
         compiler_params=pltpu.CompilerParams(vmem_limit_bytes=56 * 1024 * 1024),

time: 120 us -> 62.5 us (0.52)
  Pallas kernels: 119 us -> 61.7 us
    pallas_call x1, Pallas kernels: 66.8 us -> 8.84 us  [body(): pl.pallas_call(functools.partial(result_kernel, slab), out_shape=(jax.Sha...]
where the time goes in v3:
time: 62.5 us; the launch traced here: 62.3 us
  Pallas kernels  61.7 us (99%)
  between operations  0.64 us (1%)
    pallas_call x1, Pallas kernels, body(): pl.pallas_call(functools.partial(layer_kernel, sizes), out_shape=(jax.Sha...  52.8 us
    pallas_call x1, Pallas kernels, body(): pl.pallas_call(functools.partial(result_kernel, slab), out_shape=(jax.Sha...  8.84 us

profile of v3, /device:TPU:0, one launch (start us, length us, event | category | flops | bytes accessed | tf_op | source)
XLA Modules:
  0.0 62.3 jit_solution(12909011891406651991)
XLA Ops:
  0.6 52.8 %shard_map.158 = (bf16[2,8,32,128]{3,2,1,0:T(8,128)(2,1)}, bf16[128,4096]{1,0:T(8,128)(2,1)}, f32[32,8,2048]{2,1,0:T(8,128)}, bf16[128,128]{1,0:T(8,128)(2,1)}) custom-call(bf16[4096,128]{1,0:T(8,128)(2,1)} %bitcast.4, bf16[4096,128]{1,0:T(8,128)(2,1)} %bitcast.5, bf16[32,8,2048]{2,1,0:T(8,128)(2,1)} %weights_hbm.1, bf16[32,32]{1,0:T(8,128)(2,1)} %pointwise.1, ...), custom_call_target="tpu_custom_call" | custom-call | tf_op jit(solution)/shard_map/pallas_call | solution.py:698
  53.5 8.8 %shard_map.159 = (bf16[4096,128]{1,0:T(8,128)(2,1)}, f32[32,8,2048]{2,1,0:T(8,128)}) custom-call(bf16[2,8,32,128]{3,2,1,0:T(8,128)(2,1)} %get-tuple-element.8.arrived, bf16[128,128]{1,0:T(8,128)(2,1)} %get-tuple-element.9.mix_back, bf16[512,512]{1,0:T(8,128)(2,1)} %constant.22.clone.regroup_hbm.regroup, bf16[128,4096]{1,0:T(8,128)(2,1)} %get-tuple-element.10.delta_hbm, ...), custom_call_target="tpu_custom_call" | custom-call | tf_op jit(solution)/shard_map/pallas_call | solution.py:756

commit v4 on v3

--- a/solution.py
+++ b/solution.py
@@ -279,7 +279,7 @@
     regroup_hbm, spread_hbm, gather_hbm, tile_hbm, untile_hbm, repeat, doubling, line,
     out_cells, out_delta, out_grads, mix_back,
     cot, weights, analysis, synthesis, regroup, spread, gather, tile, untile, grads,
-    natural, rows_in, linear, upstream, delta, coarse_acc, volume, mix_fwd, bias,
+    rows_in, linear, upstream, delta, coarse_acc, volume, mix_fwd, bias,
     stack, parts, spec_wide, adj_wide, products, pulled, cells,
     space_send, space_recv, dp_send, dp_recv,
     load_sem, analysis_sem, space_ssem, space_rsem, dp_ssem, dp_rsem,
@@ -288,11 +288,10 @@
     lanes = quads * channels
     rows = 2 * kept * owners
     cell_rows = channels * slab
-    width = feats.shape[1]
+    width = feats.shape[2]
     cells_count = span_y * width
     chunk = analysis_hbm.shape[0] // analysis_sem.shape[0]
     chunks = cells_count // chunk
-    lines = chunk // width
     near = tiles // HALVES
     group = blocks * 2 * near
     part_columns = quads * group
@@ -334,19 +333,15 @@
                 barrier, inc=1, device_id={axis: lax.rem(me + step, count)}, device_id_type=mesh_id
             )
 
-    def widen(source):
+    def to_lines(source, target):
         def some(step, _):
-            at = pl.ds(pl.multiple_of(step * 512, 512), 512)
-            natural[at, :] = source[at, :].astype(f32)
+            at = pl.ds(pl.multiple_of(step * 16, 16), 16)
+            swapped = jnp.swapaxes(source[at].astype(f32), 0, 1)
+            for y in range(span_y):
+                target[at, y * width : (y + 1) * width] = swapped[y].astype(target.dtype)
             return 0
 
-        lax.fori_loop(0, natural.shape[0] // 512, some, 0)
-
-    def plane_lines(step):
-        return jnp.concatenate(
-            [natural[pl.ds(step * lines + u, cell_rows, stride=span_y), :] for u in range(lines)],
-            axis=1,
-        )
+        lax.fori_loop(0, cell_rows // 16, some, 0)
 
     def columns(step):
         return pl.ds(pl.multiple_of(step * chunk, chunk), chunk)
@@ -425,9 +420,7 @@
             weights[m, :, square + lo : square + lo + 128].astype(f32),
         )
 
-    widen(feats)
-    for step in range(chunks):
-        rows_in[:, step * chunk : (step + 1) * chunk] = plane_lines(step).astype(bf16)
+    to_lines(feats, rows_in)
 
     def analyse(half, source):
         at = slice(half * part_columns, (half + 1) * part_columns)
@@ -457,12 +450,11 @@
         repeat[...].astype(f32) * biases[...].astype(f32), axis=1, keepdims=True
     )
     load_cot.wait()
-    widen(cot)
+    to_lines(cot, upstream)
 
     def prepare(step, _):
         at = columns(step)
         linear[:, at] = dot(mix_fwd[...], rows_in[:, at]) + bias[...]
-        upstream[:, at] = plane_lines(step)
         return 0
 
     lax.fori_loop(0, chunks, prepare, 0)
@@ -616,14 +608,12 @@
 def result_kernel(
     slab, arrived, mix_back, regroup, delta_hbm, grads_hbm, synthesis_hbm,
     out_input, out_spectral,
-    delta, grads, synthesis, volume, natural, sems, synthesis_sem,
+    delta, grads, synthesis, volume, lined, natural, sems, synthesis_sem, out_sem,
 ):
     cell_rows, cells_count = delta.shape
     chunks = synthesis_sem.shape[0]
     chunk = cells_count // chunks
-    width = natural.shape[1]
-    lines = chunk // width
-    span_y = cells_count // width
+    span_y, width = natural.shape[1:]
     load_delta = pltpu.make_async_copy(delta_hbm, delta, sems.at[0])
     load_delta.start()
     loads = [
@@ -641,25 +631,43 @@
     for half in range(HALVES):
         collect_volume(slab, half, arrived.at[half], regroup, volume, None)
     load_delta.wait()
-    for step in range(chunks):
-        loads[step].wait()
-        at = slice(step * chunk, (step + 1) * chunk)
-        grad = dot(volume[...], synthesis[:, at]) + dot(mix_back[...], delta[:, at])
-        for u in range(lines):
-            natural[pl.ds(step * lines + u, cell_rows, stride=span_y), :] = grad[
-                :, u * width : (u + 1) * width
-            ]
-    load_grads.wait()
-    store_grads = pltpu.make_async_copy(grads, out_spectral, sems.at[2])
-    store_grads.start()
-
-    def narrow(step, _):
-        at = pl.ds(pl.multiple_of(step * 512, 512), 512)
-        out_input[at, :] = natural[at, :].astype(bf16)
-        return 0
-
-    lax.fori_loop(0, natural.shape[0] // 512, narrow, 0)
-    store_grads.wait()
+    parts = out_sem.shape[0]
+    part_y = span_y // parts
+    stores = []
+    for part in range(parts):
+        for step in range(part * chunks // parts, (part + 1) * chunks // parts):
+            loads[step].wait()
+            at = slice(step * chunk, (step + 1) * chunk)
+            lined[:, at] = dot(volume[...], synthesis[:, at]) + dot(mix_back[...], delta[:, at])
+
+        def swap(step, _, part=part):
+            at = pl.ds(pl.multiple_of(step * 8, 8), 8)
+            stacked = jnp.stack(
+                [
+                    lined[at, y * width : (y + 1) * width]
+                    for y in range(part * part_y, (part + 1) * part_y)
+                ],
+                axis=0,
+            )
+            natural[at, part * part_y : (part + 1) * part_y, :] = jnp.swapaxes(
+                stacked, 0, 1
+            ).astype(bf16)
+            return 0
+
+        lax.fori_loop(0, cell_rows // 8, swap, 0)
+        copy = pltpu.make_async_copy(
+            natural.at[:, pl.ds(part * part_y, part_y), :],
+            out_input.at[:, pl.ds(part * part_y, part_y), :],
+            out_sem.at[part],
+        )
+        copy.start()
+        stores.append(copy)
+        if part == 0:
+            load_grads.wait()
+            store_grads = pltpu.make_async_copy(grads, out_spectral, sems.at[2])
+            store_grads.start()
+            stores.append(store_grads)
+    wait_all(stores)
 
 
 def fits(features, spectral, owners):
@@ -667,7 +675,7 @@
     modes, kept = spectral.shape[:2]
     return (
         samples == 1 and kept == 8 and channels == 32 and slab == 4 and modes == 32
-        and span_z == 128 and span_y % 8 == 0 and (2 * kept * owners) % 16 == 0
+        and span_z == 128 and span_y % 16 == 0 and (2 * kept * owners) % 16 == 0
     )
 
 
@@ -682,7 +690,7 @@
     lanes = quads * channels
     square = channels * channels
     cell_rows, cells_count = channels * slab, span_y * span_z
-    natural_shape = (cell_rows * span_y, span_z)
+    natural_shape = (cell_rows, span_y, span_z)
     plane, doubling = np_plane_rows(span_y, span_z, blocks, tiles, quads)
     line = np_line(slab * blocks, blocks, owners)
     plane_rows = plane.shape[0]
@@ -716,7 +724,6 @@
             pltpu.VMEM(tile.shape, bf16),
             pltpu.VMEM(untile.shape, bf16),
             pltpu.VMEM(spectral.shape, f32),
-            pltpu.VMEM(natural_shape, f32),
             pltpu.VMEM((cell_rows, cells_count), bf16),
             pltpu.VMEM((cell_rows, cells_count), f32),
             pltpu.VMEM((cell_rows, cells_count), f32),
@@ -760,15 +767,17 @@
             jax.ShapeDtypeStruct(spectral.shape, f32),
         ),
         in_specs=[vmem, vmem, vmem, hbm, hbm, hbm],
-        out_specs=(vmem, hbm),
+        out_specs=(hbm, hbm),
         scratch_shapes=[
             pltpu.VMEM((cell_rows, cells_count), bf16),
             pltpu.VMEM(spectral.shape, f32),
             pltpu.VMEM((plane_rows, cells_count), bf16),
             pltpu.VMEM((cell_rows, plane_rows), bf16),
-            pltpu.VMEM(natural_shape, f32),
+            pltpu.VMEM((cell_rows, cells_count), f32),
+            pltpu.VMEM(natural_shape, bf16),
             pltpu.SemaphoreType.DMA((3,)),
             pltpu.SemaphoreType.DMA((chunks,)),
+            pltpu.SemaphoreType.DMA((span_y // 16,)),
         ],
         compiler_params=pltpu.CompilerParams(vmem_limit_bytes=56 * 1024 * 1024),
     )(arrived, mix_back, regroup, delta, grads, plane)

time: 62.5 us -> 58.9 us (0.942)
  Pallas kernels: 61.7 us -> 58.1 us
    pallas_call x1, Pallas kernels: 8.84 us -> 6.7 us  [body(): pl.pallas_call(functools.partial(result_kernel, slab), out_shape=(jax.Sha...]
    pallas_call x1, Pallas kernels: 52.8 us -> 51.4 us  [body(): pl.pallas_call(functools.partial(layer_kernel, sizes), out_shape=(jax.Sha...]
where the time goes in v4:
time: 58.9 us; the launch traced here: 58.7 us
  Pallas kernels  58.1 us (99%)
  between operations  0.64 us (1%)
    pallas_call x1, Pallas kernels, body(): pl.pallas_call(functools.partial(layer_kernel, sizes), out_shape=(jax.Sha...  51.4 us
    pallas_call x1, Pallas kernels, body(): pl.pallas_call(functools.partial(result_kernel, slab), out_shape=(jax.Sha...  6.7 us

profile of v4, /device:TPU:0, one launch (start us, length us, event | category | flops | bytes accessed | tf_op | source)
XLA Modules:
  0.0 58.7 jit_solution(3511301627001627462)
XLA Ops:
  0.6 51.4 %shard_map.158 = (bf16[2,8,32,128]{3,2,1,0:T(8,128)(2,1)}, bf16[128,4096]{1,0:T(8,128)(2,1)}, f32[32,8,2048]{2,1,0:T(8,128)}, bf16[128,128]{1,0:T(8,128)(2,1)}) custom-call(bf16[128,32,128]{2,1,0:T(8,128)(2,1)} %bitcast.4, bf16[128,32,128]{2,1,0:T(8,128)(2,1)} %bitcast.5, bf16[32,8,2048]{2,1,0:T(8,128)(2,1)} %weights_hbm.1, bf16[32,32]{1,0:T(8,128)(2,1)} %pointwise.1, ...), custom_call_target="tpu_custom_call" | custom-call | tf_op jit(solution)/shard_map/pallas_call | solution.py:706
  52.0 6.7 %shard_map.159 = (bf16[128,32,128]{2,1,0:T(8,128)(2,1)}, f32[32,8,2048]{2,1,0:T(8,128)}) custom-call(bf16[2,8,32,128]{3,2,1,0:T(8,128)(2,1)} %get-tuple-element.8.arrived, bf16[128,128]{1,0:T(8,128)(2,1)} %get-tuple-element.9.mix_back, bf16[512,512]{1,0:T(8,128)(2,1)} %constant.22.clone.regroup_hbm.regroup, bf16[128,4096]{1,0:T(8,128)(2,1)} %get-tuple-element.10.delta_hbm, ...), custom_call_target="tpu_custom_call" | custom-call | tf_op jit(solution)/shard_map/pallas_call | solution.py:763

commit v5 on v4

--- a/solution.py
+++ b/solution.py
@@ -273,6 +273,11 @@
         copy.wait()
 
 
+def wait_arrivals(copies):
+    for copy in copies:
+        copy.wait_recv()
+
+
 def layer_kernel(
     sizes,
     feats, cot_hbm, weights_hbm, pointwise, biases, analysis_hbm, synthesis_hbm,
@@ -346,16 +351,23 @@
     def columns(step):
         return pl.ds(pl.multiple_of(step * chunk, chunk), chunk)
 
+    sent = []
+
+    def sending(*exchange):
+        copies = start_exchange(*exchange)
+        sent.extend(copies)
+        return copies
+
     def send_space(turn, half):
         at = turn * HALVES + half
-        return start_exchange(
+        return sending(
             "space", blocks, space_send.at[at], space_recv.at[at],
             space_ssem.at[at], space_rsem.at[at],
         )
 
     def send_dp(turn, half):
         at = turn * HALVES + half
-        return start_exchange(
+        return sending(
             "dp", owners, dp_send.at[at], dp_recv.at[at], dp_ssem.at[at], dp_rsem.at[at]
         )
 
@@ -373,7 +385,7 @@
     def cells_to_modes(turn, dp_turn, arriving):
         copies = []
         for half in range(HALVES):
-            wait_all(arriving[half])
+            wait_arrivals(arriving[half])
             cells[half] = space_recv[turn * HALVES + half].astype(f32).reshape(cells.shape[1:])
             wide = jnp.concatenate(
                 [cells[half, pl.ds(t, blocks * 2 * slab, stride=near), :] for t in range(near)],
@@ -387,7 +399,7 @@
     def modes_to_cells(dp_turn, turn, arriving):
         copies = []
         for half in range(HALVES):
-            wait_all(arriving[half])
+            wait_arrivals(arriving[half])
             wide = dp_recv[dp_turn * HALVES + half].reshape(rows, near * lanes)
             back = lax.dot_general(line[...], wide, TN, preferred_element_type=f32)
             for t in range(near):
@@ -452,20 +464,21 @@
     load_cot.wait()
     to_lines(cot, upstream)
 
+    copies = cells_to_modes(0, 0, copies)
+
     def prepare(step, _):
         at = columns(step)
         linear[:, at] = dot(mix_fwd[...], rows_in[:, at]) + bias[...]
         return 0
 
     lax.fori_loop(0, chunks, prepare, 0)
-    copies = cells_to_modes(0, 0, copies)
     load_weights.wait()
     for copy in load_tables[1:]:
         copy.wait()
 
     back_copies = []
     for half in range(HALVES):
-        wait_all(copies[half])
+        wait_arrivals(copies[half])
         stack_half(0, half)
 
         def mix(j, _, half=half):
@@ -494,7 +507,7 @@
     copies = modes_to_cells(1, 1, back_copies)
     load_synthesis.wait()
     for half in range(HALVES):
-        wait_all(copies[half])
+        wait_arrivals(copies[half])
         collect_volume(
             slab, half, space_recv.at[HALVES + half], regroup, volume, doubling
         )
@@ -516,7 +529,7 @@
 
     back_copies = []
     for half in range(HALVES):
-        wait_all(copies[half])
+        wait_arrivals(copies[half])
         stack_half(2, half)
         wide = dot(stack[...], untile[...])
         for j in range(quads):
@@ -577,10 +590,12 @@
     store_grads.start()
     copies = modes_to_cells(3, 3, back_copies)
     for half in range(HALVES):
-        wait_all(copies[half])
+        wait_arrivals(copies[half])
         out_cells[half] = space_recv[3 * HALVES + half]
     store_delta.wait()
     store_grads.wait()
+    for copy in sent:
+        copy.wait_send()
 
 
 def collect_volume(slab, half, arrived, regroup, volume, doubling):
@@ -779,7 +794,7 @@
             pltpu.SemaphoreType.DMA((chunks,)),
             pltpu.SemaphoreType.DMA((span_y // 16,)),
         ],
-        compiler_params=pltpu.CompilerParams(vmem_limit_bytes=56 * 1024 * 1024),
+        compiler_params=pltpu.CompilerParams(vmem_limit_bytes=20 * 1024 * 1024),
     )(arrived, mix_back, regroup, delta, grads, plane)
     return grad_input.reshape(features.shape), grad_spectral
 

time: 58.9 us -> 62.3 us (1.058)
  local copies, waits for them, and re-layouts: 0 us -> 4.48 us
  Pallas kernels: 58.1 us -> 56.8 us
    unnamed x0 -> x12, local copies, waits for them, and re-layouts: none -> 4.48 us
    pallas_call x1, Pallas kernels: 6.7 us -> 5.35 us  [body(): pl.pallas_call(functools.partial(result_kernel, slab), out_shape=(jax.Sha...]
where the time goes in v5:
time: 62.3 us; the launch traced here: 62 us
  Pallas kernels  56.8 us (91%)
  local copies, waits for them, and re-layouts  4.48 us (7%)
  between operations  0.68 us (1%)
    pallas_call x1, Pallas kernels, body(): pl.pallas_call(functools.partial(layer_kernel, sizes), out_shape=(jax.Sha...  51.5 us
    pallas_call x1, Pallas kernels, body(): pl.pallas_call(functools.partial(result_kernel, slab), out_shape=(jax.Sha...  5.35 us
    unnamed x12, local copies, waits for them, and re-layouts  4.48 us

profile of v5, /device:TPU:0, one launch (start us, length us, event | category | flops | bytes accessed | tf_op | source)
XLA Modules:
  0.0 62.0 jit_solution(12235008724903330688)
XLA Ops:
  0.6 0.0 copy-start
  0.6 0.0 copy-start.1
  0.7 51.5 %shard_map.158 = (bf16[2,8,32,128]{3,2,1,0:T(8,128)(2,1)}, bf16[128,4096]{1,0:T(8,128)(2,1)}, f32[32,8,2048]{2,1,0:T(8,128)}, bf16[128,128]{1,0:T(8,128)(2,1)}) custom-call(bf16[128,32,128]{2,1,0:T(8,128)(2,1)} %bitcast.4, bf16[128,32,128]{2,1,0:T(8,128)(2,1)} %bitcast.5, bf16[32,8,2048]{2,1,0:T(8,128)(2,1)} %weights_hbm.1, bf16[32,32]{1,0:T(8,128)(2,1)} %pointwise.1, ...), custom_call_target="tpu_custom_call" | custom-call | tf_op jit(solution)/shard_map/pallas_call | solution.py:721
  52.2 0.0 copy-done
  52.2 0.0 copy-done.1
  52.2 0.0 copy-start.2
  52.2 1.6 %copy-done.2 = f32[32,8,2048]{2,1,0:T(8,128)S(1)} copy-done((f32[32,8,2048]{2,1,0:T(8,128)S(1)}, f32[32,8,2048]{2,1,0:T(8,128)}, u32[]{:S(2)}) %copy-start.2) | copy-done | bytes 2097176
  53.8 0.0 copy-start.3
  53.8 1.2 %copy-done.3 = bf16[128,4096]{1,0:T(8,128)(2,1)S(1)} copy-done((bf16[128,4096]{1,0:T(8,128)(2,1)S(1)}, bf16[128,4096]{1,0:T(8,128)(2,1)}, u32[]{:S(2)}) %copy-start.3) | copy-done | bytes 1048600
  55.0 0.0 copy-start.4
  55.0 0.9 %copy-done.4 = bf16[2,8,32,128]{3,2,1,0:T(8,128)(2,1)S(1)} copy-done((bf16[2,8,32,128]{3,2,1,0:T(8,128)(2,1)S(1)}, bf16[2,8,32,128]{3,2,1,0:T(8,128)(2,1)}, u32[]{:S(2)}) %copy-start.4) | copy-done | bytes 131096
  55.9 0.0 copy-start.5
  55.9 0.8 %copy-done.5 = bf16[128,128]{1,0:T(8,128)(2,1)S(1)} copy-done((bf16[128,128]{1,0:T(8,128)(2,1)S(1)}, bf16[128,128]{1,0:T(8,128)(2,1)}, u32[]{:S(2)}) %copy-start.5) | copy-done | bytes 32792
  56.7 5.4 %shard_map.159 = (bf16[128,32,128]{2,1,0:T(8,128)(2,1)}, f32[32,8,2048]{2,1,0:T(8,128)}) custom-call(bf16[2,8,32,128]{3,2,1,0:T(8,128)(2,1)S(1)} %copy-done.4, bf16[128,128]{1,0:T(8,128)(2,1)S(1)} %copy-done.5, bf16[512,512]{1,0:T(8,128)(2,1)S(1)} %copy-done.1, bf16[128,4096]{1,0:T(8,128)(2,1)S(1)} %copy-done.3, f32[32,8,2048]{2,1,0:T(8,128)S(1)} %copy-done.2, ...), custom_call_target="tpu_custom_call" | custom-call | tf_op jit(solution)/shard_map/pallas_call | solution.py:778
Async XLA Ops:
  0.6 51.5 %copy-start = (bf16[512,4096]{1,0:T(8,128)(2,1)S(1)}, bf16[512,4096]{1,0:T(8,128)(2,1)}, u32[]{:S(2)}) copy-start(bf16[512,4096]{1,0:T(8,128)(2,1)} %constant.21.clone.synthesis_hbm) | copy-start | bytes 12582916
  0.6 51.5 %copy-start.1 = (bf16[512,512]{1,0:T(8,128)(2,1)S(1)}, bf16[512,512]{1,0:T(8,128)(2,1)}, u32[]{:S(2)}) copy-start(bf16[512,512]{1,0:T(8,128)(2,1)} %constant.22.clone.regroup_hbm.regroup) | copy-start | bytes 1572868
  52.2 1.6 %copy-start.2 = (f32[32,8,2048]{2,1,0:T(8,128)S(1)}, f32[32,8,2048]{2,1,0:T(8,128)}, u32[]{:S(2)}) copy-start(f32[32,8,2048]{2,1,0:T(8,128)} %get-tuple-element.11.grads_hbm) | copy-start | bytes 6291460
  53.8 1.2 %copy-start.3 = (bf16[128,4096]{1,0:T(8,128)(2,1)S(1)}, bf16[128,4096]{1,0:T(8,128)(2,1)}, u32[]{:S(2)}) copy-start(bf16[128,4096]{1,0:T(8,128)(2,1)} %get-tuple-element.10.delta_hbm) | copy-start | bytes 3145732
  55.0 0.9 %copy-start.4 = (bf16[2,8,32,128]{3,2,1,0:T(8,128)(2,1)S(1)}, bf16[2,8,32,128]{3,2,1,0:T(8,128)(2,1)}, u32[]{:S(2)}) copy-start(bf16[2,8,32,128]{3,2,1,0:T(8,128)(2,1)} %get-tuple-element.8.arrived) | copy-start | bytes 393220
  55.9 0.8 %copy-start.5 = (bf16[128,128]{1,0:T(8,128)(2,1)S(1)}, bf16[128,128]{1,0:T(8,128)(2,1)}, u32[]{:S(2)}) copy-start(bf16[128,128]{1,0:T(8,128)(2,1)} %get-tuple-element.9.mix_back) | copy-start | bytes 98308
